TPU v7x, 128 devices: a whole 4x4x4 slice. The times are simulated.
128 devices in a mesh: group: 16 (over y, z), tp: 8 (over x, core).
Axes of the slice: x: 4, y: 4, z: 4, core: 2. Of those that a mesh axis runs over, the one named last changes fastest.
Arguments:
- queries: bfloat16 [64, 8192], P('group', 'tp'), may hold values from -6 to 6
- incoming_keys: bfloat16 [64, 1024], P('group', 'tp'), may hold values from -10 to 10
- incoming_values: bfloat16 [64, 1024], P('group', 'tp'), may hold values from -6 to 6
- cache_keys: bfloat16 [96, 4096, 1024], P('group', None, 'tp'), may hold values from -10 to 10
- pooled_values: bfloat16 [96, 4096, 1024], P('group', None, 'tp'), may hold values from -6 to 6
- lengths: int32 [64], replicated, may hold values from 2 to 98304, as said below
- slot_request: int32 [96], P('group'), may hold values from 0 to 63, as said below
- slot_block: int32 [96], P('group'), may hold values from 0 to 23, as said below
- out_weight: bfloat16 [8192, 4096], P('tp'), may hold values from -0.0625 to 0.0625
Outputs:
- attended: bfloat16 [64, 4096], P('group', 'tp')
Inputs may be any that keep to these rules, and one draw needn't show every extreme that they name: `slot_request`: each request owns between 1 and 24 slots, one request exactly 24; every slot is used. `slot_block`: the slots of a request with c slots hold its block indices 0 to c - 1, once each, on any devices. `lengths`: A request with c slots has a length from 4096 * (c - 1) + 2 to 4096 * c; the longest is 98304.
All inputs are finite; a program needn't handle non-finite values.
Results may differ from a plain program's by a relative error of at most 0.008.
Values may be sent and summed in bfloat16 or wider, within the bound.
No kernel may reach another device: no remote copies, remote signals or barrier semaphores. Data moves between devices by JAX's collectives and lax.ppermute only.
A program may use at most 64 MiB of HBM per device.

v0:
```python
import math

import jax
import jax.numpy as jnp
from jax import lax
from jax.sharding import PartitionSpec as P

QUERY_HEADS = 64
KEY_VALUE_HEADS = 8
HEAD_SIZE = 128


def slot_partials(query_all, cache_keys, pooled_values, lengths, slot_request, slot_block):
    slot_count, block_len, kv_width = cache_keys.shape
    kv_local = kv_width // HEAD_SIZE
    heads_per_group = QUERY_HEADS // KEY_VALUE_HEADS
    chosen = query_all[slot_request].reshape(slot_count, kv_local, heads_per_group, HEAD_SIZE)
    key_row_list = cache_keys.reshape(slot_count, block_len, kv_local, HEAD_SIZE)
    value_row_list = pooled_values.reshape(slot_count, block_len, kv_local, HEAD_SIZE)
    logit_scores = jnp.einsum(
        "sgrd,stgd->sgrt", chosen, key_row_list, preferred_element_type=jnp.float32
    ) / math.sqrt(HEAD_SIZE)
    filled = jnp.clip(lengths[slot_request] - block_len * slot_block, 0, block_len)
    usable = (
        jnp.arange(block_len, dtype=jnp.int32)[None, None, None, :] < filled[:, None, None, None]
    )
    slot_peak = jnp.max(jnp.where(usable, logit_scores, -1e30), axis=3)
    rounded = jnp.where(usable, jnp.exp(logit_scores - slot_peak[..., None]), 0.0).astype(
        jnp.bfloat16
    )
    slot_total = jnp.sum(rounded.astype(jnp.float32), axis=3)
    block_weighted_values = jnp.einsum(
        "sgrt,stgd->sgrd", rounded, value_row_list, preferred_element_type=jnp.float32
    )
    head_count = kv_local * heads_per_group
    return (
        slot_peak.reshape(slot_count, head_count),
        slot_total.reshape(slot_count, head_count),
        block_weighted_values.reshape(slot_count, head_count, HEAD_SIZE),
    )


def request_sums(member_float, slot_total, block_weighted_values, factor):
    slot_count = slot_total.shape[0]
    row_sums = jnp.dot(member_float, slot_total * factor, precision=lax.Precision.HIGHEST)
    scaled = (block_weighted_values * factor[..., None]).reshape(slot_count, -1)
    row_accs = jnp.dot(member_float, scaled, precision=lax.Precision.HIGHEST)
    return (row_sums, row_accs)


def per_device(
    queries,
    incoming_keys,
    incoming_values,
    cache_keys,
    pooled_values,
    lengths,
    slot_request,
    slot_block,
    out_weight,
):
    query_all = lax.all_gather(queries, "group", axis=0, tiled=True)
    request_list = query_all.shape[0]
    home_rows = queries.shape[0]
    kv_local = incoming_keys.shape[1] // HEAD_SIZE
    heads_per_group = QUERY_HEADS // KEY_VALUE_HEADS
    head_count = kv_local * heads_per_group
    slot_peak, slot_total, block_weighted_values = slot_partials(
        query_all, cache_keys, pooled_values, lengths, slot_request, slot_block
    )
    member = slot_request[None, :] == jnp.arange(request_list, dtype=jnp.int32)[:, None]
    member_float = member.astype(jnp.float32)
    request_best = jnp.max(jnp.where(member[:, :, None], slot_peak[None], -1e30), axis=1)
    home_queries = queries.reshape(home_rows, kv_local, heads_per_group, HEAD_SIZE)
    fresh_score = jnp.einsum(
        "ngrd,ngd->ngr",
        home_queries,
        incoming_keys.reshape(home_rows, kv_local, HEAD_SIZE),
        preferred_element_type=jnp.float32,
    ).reshape(home_rows, head_count) / math.sqrt(HEAD_SIZE)
    fresh_value = (
        jnp.broadcast_to(
            incoming_values.reshape(home_rows, kv_local, 1, HEAD_SIZE),
            (home_rows, kv_local, heads_per_group, HEAD_SIZE),
        )
        .astype(jnp.float32)
        .reshape(home_rows, head_count, HEAD_SIZE)
    )
    factor = jnp.exp(slot_peak - request_best[slot_request])
    row_sums, row_accs = request_sums(member_float, slot_total, block_weighted_values, factor)
    got_best, got_sums, got_accs = (
        lax.all_to_all(request_best[None], "group", split_axis=1, concat_axis=0, tiled=True),
        lax.all_to_all(row_sums[None], "group", split_axis=1, concat_axis=0, tiled=True),
        lax.all_to_all(row_accs[None], "group", split_axis=1, concat_axis=0, tiled=True),
    )
    combined_top = jnp.maximum(jnp.max(got_best, axis=0), fresh_score)
    rescale = jnp.exp(got_best - combined_top[None])
    fresh_weight = jnp.exp(fresh_score - combined_top)
    denominator = fresh_weight + jnp.sum(rescale * got_sums, axis=0)
    sources = got_accs.shape[0]
    numerator = fresh_weight[..., None] * fresh_value + jnp.sum(
        rescale[..., None] * got_accs.reshape(sources, home_rows, head_count, HEAD_SIZE), axis=0
    )
    attention = (
        (numerator / denominator[..., None])
        .astype(jnp.bfloat16)
        .reshape(home_rows, head_count * HEAD_SIZE)
    )
    partial_value = jnp.dot(attention, out_weight, preferred_element_type=jnp.float32)
    return lax.psum_scatter(partial_value, "tp", scatter_dimension=1, tiled=True).astype(
        jnp.bfloat16
    )


def solution(mesh):
    placed = (
        P("group", "tp"),
        P("group", "tp"),
        P("group", "tp"),
        P("group", None, "tp"),
        P("group", None, "tp"),
        P(),
        P("group"),
        P("group"),
        P("tp", None),
    )
    return jax.shard_map(
        per_device, mesh=mesh, in_specs=placed, out_specs=P("group", "tp"), check_vma=False
    )
```

profile of v0, /device:TPU:0, one launch (start us, length us, event | category | flops | bytes accessed | tf_op | source)
XLA Modules:
  0.0 128.8 jit_solution(12659258255783426018)
XLA Ops:
  6.5 0.7 compare_select_fusion
  7.2 0.7 iota_compare_fusion.1
  7.9 1.3 %gather_fusion = s32[6]{0:T(128)S(1)} fusion(s32[64]{0:T(128)} %param.14, s32[1024]{0:T(1024)S(1)} %pad_clamp_fusion), kind=kCustom, calls=%fused_computation | custom fusion | bytes 72 | tf_op jit(solution)/shard_map/gather | solution.py:23
  9.2 0.7 subtract_clamp_fusion
  10.0 25.2 %all-gather = bf16[16,4,1024]{2,1,0:T(4,128)(2,1)S(1)} all-gather(bf16[1,4,1024]{2,1,0:T(4,128)(2,1)} %bitcast.46), channel_id=1, replica_groups=mesh['group'=16,'tp'=8] {'group'}, dimensions={0}, use_global_device_ids=true | all-gather | bytes 139264 | tf_op jit(solution)/shard_map/all_gather | solution.py:62
  35.3 0.6 gather_fusion.1
  35.8 4.6 %select_reduce_fusion = (f32[6,8]{1,0:T(8,128)S(1)}, f32[6,8,4096]{2,1,0:T(8,128)S(1)}) fusion(pred[6,4096]{1,0:T(8,128)(4,1)S(1)} %iota_compare_fusion, bf16[6,4096,128]{2,1,0:T(8,128)(2,1)} %param.12, bf16[1,6,8,128]{3,1,2,0:T(8,128)(2,1)S(1)} %bitcast.44), kind=kOutput, calls=%fused_computation.10 | convolution fusion | flops 50921424 | bytes 7114944 | tf_op jit(solution)/shard_map/sgrd,stgd->sgrt/dot_general | solution.py:20
  40.5 0.7 copy.18
  41.2 4.9 %all-to-all-start = ((f32[1,64,8]{2,0,1:T(1,128)}), f32[1,64,8]{2,0,1:T(1,128)S(1)}, u32[]{:S(2)}, u32[]{:S(2)}) async-start(f32[1,64,8]{2,0,1:T(1,128)} %copy.18), calls=%async_computation | async-start | bytes 65536 | tf_op jit(solution)/shard_map/all_to_all | solution.py:92
  46.3 0.3 convert_reduce_fusion
  46.6 0.6 gather_fusion.2
  47.1 3.8 %fusion = f32[1,6,8,128]{3,2,1,0:T(8,128)S(1)} fusion(bf16[6,4096,128]{2,1,0:T(8,128)(2,1)} %param.13, f32[6,8,4096]{2,1,0:T(8,128)S(1)} %get-tuple-element.10, f32[6,8]{1,0:T(8,128)S(1)} %get-tuple-element.9, pred[6,4096]{1,0:T(8,128)(4,1)S(1)} %iota_compare_fusion, f32[6,8]{1,0:T(8,128)S(1)} %subtract_exponential_fusion.1), kind=kOutput, calls=%fused_computation.7 | convolution fusion | flops 50927616 | bytes 7127424 | tf_op jit(solution)/shard_map/sgrt,stgd->sgrd/dot_general | solution.py:32
  51.0 0.9 fusion.11
  52.0 0.4 convolution_bitcast_fusion.1
  52.4 1.0 copy.20
  53.4 0.4 all-to-all-done
  53.8 6.8 %all-to-all-start.2 = ((f32[1,64,8]{2,0,1:T(1,128)}), f32[1,64,8]{2,0,1:T(1,128)S(1)}, u32[]{:S(2)}, u32[]{:S(2)}) async-start(f32[1,64,8]{2,0,1:T(1,128)} %bitcast.12), calls=%async_computation.2 | async-start | bytes 65536 | tf_op jit(solution)/shard_map/all_to_all | solution.py:93
  60.6 7.7 %all-to-all-done.2 = f32[1,64,8]{2,0,1:T(1,128)S(1)} async-done(((f32[1,64,8]{2,0,1:T(1,128)}), f32[1,64,8]{2,0,1:T(1,128)S(1)}, u32[]{:S(2)}, u32[]{:S(2)}) %all-to-all-start.2) | async-done | bytes 2080 | tf_op jit(solution)/shard_map/all_to_all | solution.py:93
  68.3 3.5 %all-to-all-start.1 = ((f32[1,64,1024]{2,0,1:T(1,128)}), f32[1,64,1024]{2,0,1:T(1,128)S(1)}, u32[]{:S(2)}, u32[]{:S(2)}) async-start(f32[1,64,1024]{2,0,1:T(1,128)} %copy.20), calls=%async_computation.1 | async-start | bytes 524288 | tf_op jit(solution)/shard_map/all_to_all | solution.py:94
  72.0 8.3 %all-to-all-done.1 = f32[1,64,1024]{2,0,1:T(1,128)S(1)} async-done(((f32[1,64,1024]{2,0,1:T(1,128)}), f32[1,64,1024]{2,0,1:T(1,128)S(1)}, u32[]{:S(2)}, u32[]{:S(2)}) %all-to-all-start.1) | async-done | bytes 262176 | tf_op jit(solution)/shard_map/all_to_all | solution.py:94
  80.3 0.1 multiply_reduce_fusion
  80.5 8.1 %convolution_bitcast_fusion = f32[4096,4]{1,0:T(8,128)} fusion(bf16[1024,4096]{1,0:T(8,128)(2,1)} %param.17, bf16[1,4,8,128]{3,2,1,0:T(8,128)(2,1)S(1)} %fusion.10), kind=kOutput, calls=%fused_computation.3 | convolution fusion | flops 33554432 | bytes 8462336
  88.7 31.7 %reduce-scatter.4.cloned.1.call-done = f32[512,4]{1,0:T(8,128)} async-done(((f32[4096,4]{1,0:T(8,128)}), f32[512,4]{1,0:T(8,128)}) %reduce-scatter.4.cloned.1.call-update) | async-done | bytes 8208
  120.3 1.7 %copy.25 = bf16[4,512]{1,0:T(4,128)(2,1)} copy(f32[4,512]{0,1:T(8,128)} %bitcast.42) | data formatting | bytes 12288
  (23 shorter events, 0.7 us)
Async XLA Ops:
  6.5 45.3 %copy-start = (bf16[4,128]{1,0:T(4,128)(2,1)S(1)}, bf16[4,128]{1,0:T(4,128)(2,1)}, u32[]{:S(2)}) copy-start(bf16[4,128]{1,0:T(4,128)(2,1)} %param.10) | copy-start | bytes 3076
  41.2 12.6 %all-to-all-start = ((f32[1,64,8]{2,0,1:T(1,128)}), f32[1,64,8]{2,0,1:T(1,128)S(1)}, u32[]{:S(2)}, u32[]{:S(2)}) async-start(f32[1,64,8]{2,0,1:T(1,128)} %copy.18), calls=%async_computation | async-start | bytes 65536 | tf_op jit(solution)/shard_map/all_to_all | solution.py:92
  46.2 4.7 %copy-start.3 = (s32[6]{0:T(128)S(1)}, s32[6]{0:T(128)}, u32[]{:S(2)}) copy-start(s32[6]{0:T(128)} %param.15) | copy-start | bytes 76
  46.2 5.6 %copy-start.1 = (bf16[4,1024]{1,0:T(4,128)(2,1)S(1)}, bf16[4,1024]{1,0:T(4,128)(2,1)}, u32[]{:S(2)}) copy-start(bf16[4,1024]{1,0:T(4,128)(2,1)} %param.9) | copy-start | bytes 24580
  46.6 5.8 %copy-start.2 = (bf16[4,128]{1,0:T(4,128)(2,1)S(1)}, bf16[4,128]{1,0:T(4,128)(2,1)}, u32[]{:S(2)}) copy-start(bf16[4,128]{1,0:T(4,128)(2,1)} %param.11) | copy-start | bytes 3076
  53.8 14.6 %all-to-all-start.2 = ((f32[1,64,8]{2,0,1:T(1,128)}), f32[1,64,8]{2,0,1:T(1,128)S(1)}, u32[]{:S(2)}, u32[]{:S(2)}) async-start(f32[1,64,8]{2,0,1:T(1,128)} %bitcast.12), calls=%async_computation.2 | async-start | bytes 65536 | tf_op jit(solution)/shard_map/all_to_all | solution.py:93
  68.3 12.0 %all-to-all-start.1 = ((f32[1,64,1024]{2,0,1:T(1,128)}), f32[1,64,1024]{2,0,1:T(1,128)S(1)}, u32[]{:S(2)}, u32[]{:S(2)}) async-start(f32[1,64,1024]{2,0,1:T(1,128)} %copy.20), calls=%async_computation.1 | async-start | bytes 524288 | tf_op jit(solution)/shard_map/all_to_all | solution.py:94
  71.9 48.5 %reduce-scatter.4.cloned.1.call-start = ((), (), s32[]{:S(2)}) async-start(), calls=%async_computation.4 | async-start | bytes 2359296
Sparse Core Ops, SparseCore 0:
  88.8 31.5 reduce-scatter.3
where the time goes:
time: 129 us
  waiting for transfers between devices  48.1 us (37%)
  blocking collectives  25.2 us (20%)
  matrix products  17.9 us (14%)
  starting transfers between devices  15.3 us (12%)
  between operations  13.5 us (10%)
  local copies, waits for them, and re-layouts  5.87 us (5%)
  other arithmetic  2.87 us (2%)
    unnamed x2, waiting for transfers between devices  31.7 us
    all_gather x1, blocking collectives, per_device(): query_all = lax.all_gather(queries, 'group', axis=0, tiled=True)  25.2 us
    all_to_all x1, waiting for transfers between devices, per_device(): lax.all_to_all(row_accs[None], 'group', split_axis=1, concat_axis=0, tile...  8.34 us
    unnamed x1, matrix products  8.1 us
    all_to_all x1, waiting for transfers between devices, per_device(): lax.all_to_all(row_sums[None], 'group', split_axis=1, concat_axis=0, tile...  7.69 us
    all_to_all x1, starting transfers between devices, per_device(): lax.all_to_all(row_sums[None], 'group', split_axis=1, concat_axis=0, tile...  6.82 us
    all_to_all x1, starting transfers between devices, per_device(): lax.all_to_all(request_best[None], 'group', split_axis=1, concat_axis=0,...  4.94 us
    dot_general x1, matrix products, slot_partials(): jnp.einsum('sgrd,stgd->sgrt', chosen, key_row_list, preferred_element_typ...  4.6 us
  transfers between devices with their start and end apart: 4, of which 4 were waited for; matrix products, arithmetic and copies ran while one was open for 6% of the time, Pallas kernels for 0%

commit v1 on v0

v1 whole, which is shorter than its diff:
```python
import functools
import math

import jax
import jax.numpy as jnp
from jax import lax
from jax.experimental import pallas as pl
from jax.experimental.pallas import tpu as pltpu
from jax.sharding import PartitionSpec as P

HEAD = 128
HEADS = 8
LOW = -1e30
MIB = 1024 * 1024
STAT_ROWS = 8


def same_lane(shape):
    row = lax.broadcasted_iota(jnp.int32, shape, len(shape) - 2)
    lane = lax.broadcasted_iota(jnp.int32, shape, len(shape) - 1)
    return row, lane


def partials_kernel(req_ref, blk_ref, len_ref, q_ref, k_ref, v_ref, out_ref, rows, sums, stats):
    homes, per_home, width = q_ref.shape
    slots, tokens, _ = k_ref.shape
    for i in range(homes):
        rows[per_home * i : per_home * (i + 1), :] = q_ref[i].astype(jnp.float32)
    sums[...] = jnp.zeros_like(sums)
    stats[...] = jnp.full_like(stats, LOW)
    token = lax.broadcasted_iota(jnp.int32, (HEADS, tokens), 1)
    reqs, peaks, totals, accs = [], [], [], []
    for s in range(slots):
        r = req_ref[s]
        filled = jnp.clip(len_ref[r] - tokens * blk_ref[s], 0, tokens)
        row = rows[pl.ds(r, 1), :]
        q = jnp.concatenate([row[:, HEAD * h : HEAD * (h + 1)] for h in range(HEADS)], axis=0)
        score = lax.dot_general(
            q.astype(jnp.bfloat16), k_ref[s], (((1,), (1,)), ((), ())),
            preferred_element_type=jnp.float32,
        ) * (1.0 / math.sqrt(HEAD))
        usable = token < filled
        score = jnp.where(usable, score, LOW)
        peak = jnp.max(score, axis=1, keepdims=True)
        prob = jnp.where(usable, jnp.exp(score - peak), 0.0).astype(jnp.bfloat16)
        total = jnp.sum(prob.astype(jnp.float32), axis=1, keepdims=True)
        acc = jnp.dot(prob, v_ref[s], preferred_element_type=jnp.float32)
        reqs.append(r)
        peaks.append(jnp.broadcast_to(peak, (HEADS, HEAD)))
        totals.append(jnp.broadcast_to(total, (HEADS, HEAD)))
        accs.append(acc)
    tops = []
    for s in range(slots):
        top = peaks[s]
        for o in range(slots):
            if o != s:
                top = jnp.where(reqs[o] == reqs[s], jnp.maximum(top, peaks[o]), top)
        tops.append(top)
    weights = [jnp.exp(peaks[s] - tops[s]) for s in range(slots)]
    totals = [weights[s] * totals[s] for s in range(slots)]
    accs = [weights[s] * accs[s] for s in range(slots)]
    for s in range(slots):
        total, acc = totals[s], accs[s]
        for o in range(slots):
            if o != s:
                same = reqs[o] == reqs[s]
                total = total + jnp.where(same, totals[o], 0.0)
                acc = acc + jnp.where(same, accs[o], 0.0)
        sums[reqs[s]] = acc / total
        stats[reqs[s]] = tops[s] + jnp.log(total)
    cells = per_home * HEADS
    out_ref[:, :cells, :] = sums[...].reshape(homes, cells, HEAD).astype(jnp.bfloat16)
    row, lane = same_lane((homes, cells, HEAD))
    picked = jnp.sum(
        jnp.where(lane % cells == row, stats[...].reshape(homes, cells, HEAD), 0.0),
        axis=1, keepdims=True,
    )
    high = picked.astype(jnp.bfloat16).astype(jnp.float32)
    rest = picked - high
    middle = rest.astype(jnp.bfloat16).astype(jnp.float32)
    low = rest - middle
    part = lax.broadcasted_iota(jnp.int32, picked.shape, 2) // cells
    coded = jnp.where(part == 0, high, jnp.where(part == 1, middle, jnp.where(part == 2, low, 0.0)))
    out_ref[:, cells:, :] = jnp.broadcast_to(coded, (homes, STAT_ROWS, HEAD)).astype(jnp.bfloat16)


def combine_kernel(got_ref, q_ref, key_ref, value_ref, w_ref, out_ref, rows):
    homes = got_ref.shape[0]
    mine = q_ref.shape[0]
    cells = mine * HEADS
    row, lane = same_lane((homes, cells, HEAD))
    coded = jnp.broadcast_to(
        got_ref[:, cells : cells + 1, :].astype(jnp.float32), (homes, cells, HEAD)
    )
    spread = jnp.where((lane % cells == row) & (lane < 3 * cells), coded, 0.0)
    lse = jnp.dot(
        spread.astype(jnp.bfloat16).reshape(homes * cells, HEAD),
        jnp.ones((HEAD, HEAD), jnp.bfloat16),
        preferred_element_type=jnp.float32,
    ).reshape(homes, cells, HEAD)
    for h in range(HEADS):
        rows[pl.ds(h, mine, stride=HEADS), :] = q_ref[:, HEAD * h : HEAD * (h + 1)].astype(
            jnp.float32
        )
    keys = key_ref[...].astype(jnp.float32)
    keys = jnp.broadcast_to(keys[:, None, :], (mine, HEADS, HEAD)).reshape(cells, HEAD)
    values = value_ref[...].astype(jnp.float32)
    values = jnp.broadcast_to(values[:, None, :], (mine, HEADS, HEAD)).reshape(cells, HEAD)
    fresh = jnp.sum(rows[...] * keys, axis=1, keepdims=True) * (1.0 / math.sqrt(HEAD))
    fresh = jnp.broadcast_to(fresh, (cells, HEAD))
    top = jnp.maximum(jnp.max(lse, axis=0), fresh)
    weight = jnp.exp(lse - top[None])
    fresh_weight = jnp.exp(fresh - top)
    total = fresh_weight + jnp.sum(weight, axis=0)
    number = fresh_weight * values + jnp.sum(
        weight * got_ref[:, :cells, :].astype(jnp.float32), axis=0
    )
    rows[...] = number / total
    attention = jnp.concatenate(
        [rows[pl.ds(h, mine, stride=HEADS), :] for h in range(HEADS)], axis=1
    ).astype(jnp.bfloat16)
    parts, _, width = out_ref.shape
    for p in range(parts):
        out_ref[p] = jnp.dot(
            attention, w_ref[:, width * p : width * (p + 1)], preferred_element_type=jnp.float32
        ).astype(out_ref.dtype)


def whole():
    return pl.BlockSpec(memory_space=pltpu.VMEM)


def per_device(
    homes, parts, queries, incoming_keys, incoming_values, cache_keys, pooled_values,
    lengths, slot_request, slot_block, out_weight,
):
    mine, width = queries.shape
    cells = mine * HEADS
    with jax.named_scope("queries_to_owners"):
        query_all = lax.all_to_all(
            jnp.broadcast_to(queries[None], (homes, mine, width)), "group", 0, 0, tiled=True
        )
    with jax.named_scope("slot_partials"):
        sent = pl.pallas_call(
            partials_kernel,
            out_shape=jax.ShapeDtypeStruct((homes, cells + STAT_ROWS, HEAD), jnp.bfloat16),
            in_specs=[pl.BlockSpec(memory_space=pltpu.SMEM)] * 3 + [whole()] * 3,
            out_specs=whole(),
            scratch_shapes=[
                pltpu.VMEM((homes * mine, width), jnp.float32),
                pltpu.VMEM((homes * mine, HEADS, HEAD), jnp.float32),
                pltpu.VMEM((homes * mine, HEADS, HEAD), jnp.float32),
            ],
            compiler_params=pltpu.CompilerParams(vmem_limit_bytes=24 * MIB),
        )(slot_request, slot_block, lengths, query_all, cache_keys, pooled_values)
    with jax.named_scope("partials_to_homes"):
        got = lax.all_to_all(sent, "group", 0, 0, tiled=True)
    with jax.named_scope("combine_and_project"):
        shares = pl.pallas_call(
            combine_kernel,
            out_shape=jax.ShapeDtypeStruct(
                (parts, mine, out_weight.shape[1] // parts), jnp.bfloat16
            ),
            in_specs=[whole()] * 5,
            out_specs=whole(),
            scratch_shapes=[pltpu.VMEM((cells, HEAD), jnp.float32)],
            compiler_params=pltpu.CompilerParams(vmem_limit_bytes=16 * MIB),
        )(got, queries, incoming_keys, incoming_values, out_weight)
    with jax.named_scope("sum_over_features"):
        shares = lax.all_to_all(shares, "tp", 0, 0, tiled=True)
        return jnp.sum(shares.astype(jnp.float32), axis=0).astype(jnp.bfloat16)


def solution(mesh):
    placed = (
        P("group", "tp"),
        P("group", "tp"),
        P("group", "tp"),
        P("group", None, "tp"),
        P("group", None, "tp"),
        P(),
        P("group"),
        P("group"),
        P("tp", None),
    )
    body = functools.partial(per_device, mesh.shape["group"], mesh.shape["tp"])
    return jax.shard_map(
        body, mesh=mesh, in_specs=placed, out_specs=P("group", "tp"), check_vma=False
    )
```

time: 129 us -> 52.4 us (0.41)
  the two profiles are of different devices: /device:TPU:0 before, /device:TPU:1 now
where the time goes in v1:
time: 52.4 us; the launch traced here: 52 us
  blocking collectives  37.3 us (71%)
  local copies, waits for them, and re-layouts  8.28 us (16%)
  Pallas kernels  5.74 us (11%)
  other arithmetic  0.62 us (1%)
    all_to_all x1, blocking collectives, per_device(): lax.all_to_all(jnp.broadcast_to(queries[None], (homes, mine, width)), 'gr...  15.3 us
    all_to_all x1, blocking collectives, per_device(): shares = lax.all_to_all(shares, 'tp', 0, 0, tiled=True)  11.9 us
    all_to_all x1, blocking collectives, per_device(): got = lax.all_to_all(sent, 'group', 0, 0, tiled=True)  10.1 us
    unnamed x18, local copies, waits for them, and re-layouts  7.55 us
    pallas_call x1, Pallas kernels, per_device(): pl.pallas_call(partials_kernel, out_shape=jax.ShapeDtypeStruct((homes, ce...  4.31 us
    pallas_call x1, Pallas kernels, per_device(): pl.pallas_call(combine_kernel, out_shape=jax.ShapeDtypeStruct((parts, min...  1.43 us

profile of v1, /device:TPU:1, one launch (start us, length us, event | category | flops | bytes accessed | tf_op | source)
XLA Modules:
  0.0 52.0 jit_solution(3006119322043818498)
XLA Ops:
  0.0 0.7 %broadcast_in_dim.2 = bf16[16,4,1024]{2,1,0:T(4,128)(2,1)S(1)} broadcast(bf16[4,1024]{1,0:T(4,128)(2,1)} %q_ref.1), dimensions={1,2} | broadcast | bytes 139264 | tf_op jit(solution)/shard_map/queries_to_owners/broadcast_in_dim | solution.py:141
  0.7 15.3 %all_to_all.15.q_ref = bf16[16,4,1024]{2,1,0:T(4,128)(2,1)S(1)} all-to-all(bf16[16,4,1024]{2,1,0:T(4,128)(2,1)S(1)} %broadcast_in_dim.2), channel_id=1, replica_groups=mesh['group'=16,'tp'=8] {'group'}, dimensions={0} | all-to-all | bytes 262144 | tf_op jit(solution)/shard_map/queries_to_owners/all_to_all | solution.py:140
  16.0 0.0 copy-start.1
  16.0 2.8 %copy-done.1 = bf16[6,4096,128]{2,1,0:T(8,128)(2,1)S(1)} copy-done((bf16[6,4096,128]{2,1,0:T(8,128)(2,1)S(1)}, bf16[6,4096,128]{2,1,0:T(8,128)(2,1)}, u32[]{:S(2)}) %copy-start.1) | copy-done | bytes 6291480
  18.8 0.0 copy-start.2
  18.8 2.8 %copy-done.2 = bf16[6,4096,128]{2,1,0:T(8,128)(2,1)S(1)} copy-done((bf16[6,4096,128]{2,1,0:T(8,128)(2,1)S(1)}, bf16[6,4096,128]{2,1,0:T(8,128)(2,1)}, u32[]{:S(2)}) %copy-start.2) | copy-done | bytes 6291480
  21.6 0.0 copy-start.6
  21.6 0.7 %copy-done.6 = s32[6]{0:T(128)S(1)} copy-done((s32[6]{0:T(128)S(1)}, s32[6]{0:T(128)}, u32[]{:S(2)}) %copy-start.6) | copy-done | bytes 48
  22.2 0.0 copy-start.7
  22.2 0.7 %copy-done.7 = s32[6]{0:T(128)S(1)} copy-done((s32[6]{0:T(128)S(1)}, s32[6]{0:T(128)}, u32[]{:S(2)}) %copy-start.7) | copy-done | bytes 48
  22.9 0.0 copy-start.8
  22.9 0.7 %copy-done.8 = s32[64]{0:T(128)S(1)} copy-done((s32[64]{0:T(128)S(1)}, s32[64]{0:T(128)}, u32[]{:S(2)}) %copy-start.8) | copy-done | bytes 280
  23.5 0.0 copy-start.3
  23.5 0.0 copy-start.4
  23.5 0.0 copy-start.5
  23.6 4.3 %slot_partials.1 = bf16[16,40,128]{2,1,0:T(8,128)(2,1)S(1)} custom-call(s32[6]{0:T(128)S(1)} %copy-done.6, s32[6]{0:T(128)S(1)} %copy-done.7, s32[64]{0:T(128)S(1)} %copy-done.8, bf16[16,4,1024]{2,1,0:T(4,128)(2,1)S(1)} %all_to_all.15.q_ref, bf16[6,4096,128]{2,1,0:T(8,128)(2,1)S(1)} %copy-done.1, bf16[6,4096,128]{2,1,0:T(8,128)(2,1)S(1)} %copy-done.2), custom_call_target="tpu_custom_call" | custom-call | tf_op jit(solution)/shard_map/slot_partials/pallas_call | solution.py:144
  27.9 10.1 %all_to_all.16.got_ref = bf16[16,40,128]{2,1,0:T(8,128)(2,1)S(1)} all-to-all(bf16[16,40,128]{2,1,0:T(8,128)(2,1)S(1)} %slot_partials.1), channel_id=1, replica_groups=mesh['group'=16,'tp'=8] {'group'}, dimensions={0} | all-to-all | bytes 327680 | tf_op jit(solution)/shard_map/partials_to_homes/all_to_all | solution.py:157
  38.0 0.0 copy-done
  38.0 0.0 copy-done.3
  38.0 0.0 copy-done.4
  38.0 0.0 copy-done.5
  38.0 1.4 %combine_and_project.1 = bf16[8,4,512]{2,1,0:T(4,128)(2,1)S(1)} custom-call(bf16[16,40,128]{2,1,0:T(8,128)(2,1)S(1)} %all_to_all.16.got_ref, bf16[4,1024]{1,0:T(4,128)(2,1)S(1)} %copy-done.3, bf16[4,128]{1,0:T(4,128)(2,1)S(1)} %copy-done.4, bf16[4,128]{1,0:T(4,128)(2,1)S(1)} %copy-done.5, bf16[1024,4096]{1,0:T(8,128)(2,1)S(1)} %copy-done), custom_call_target="tpu_custom_call" | custom-call | tf_op jit(solution)/shard_map/combine_and_project/pallas_call | solution.py:159
  39.5 11.9 %all_to_all.17 = bf16[8,4,512]{2,1,0:T(4,128)(2,1)S(1)} all-to-all(bf16[8,4,512]{2,1,0:T(4,128)(2,1)S(1)} %combine_and_project.1), channel_id=1, replica_groups=mesh['group'=16,'tp'=8] {'tp'}, dimensions={0} | all-to-all | bytes 65536 | tf_op jit(solution)/shard_map/sum_over_features/all_to_all | solution.py:170
  51.4 0.6 %reduce_sum.12 = bf16[4,512]{1,0:T(4,128)(2,1)} reduce(bf16[8,4,512]{2,1,0:T(4,128)(2,1)S(1)} %all_to_all.17, bf16[]{:T(256)} %constant.2.clone.1), dimensions={0}, to_apply=%region_0.0 | reduce | flops 14336 | bytes 36866 | tf_op jit(solution)/shard_map/sum_over_features/reduce_sum | solution.py:171
  (1 shorter events, 0.0 us)
Async XLA Ops:
  16.0 2.8 %copy-start.1 = (bf16[6,4096,128]{2,1,0:T(8,128)(2,1)S(1)}, bf16[6,4096,128]{2,1,0:T(8,128)(2,1)}, u32[]{:S(2)}) copy-start(bf16[6,4096,128]{2,1,0:T(8,128)(2,1)} %k_ref.1) | copy-start | bytes 18874372
  18.8 2.8 %copy-start.2 = (bf16[6,4096,128]{2,1,0:T(8,128)(2,1)S(1)}, bf16[6,4096,128]{2,1,0:T(8,128)(2,1)}, u32[]{:S(2)}) copy-start(bf16[6,4096,128]{2,1,0:T(8,128)(2,1)} %v_ref.1) | copy-start | bytes 18874372
  21.6 0.7 %copy-start.6 = (s32[6]{0:T(128)S(1)}, s32[6]{0:T(128)}, u32[]{:S(2)}) copy-start(s32[6]{0:T(128)} %req_ref.1) | copy-start | bytes 76
  22.2 0.7 %copy-start.7 = (s32[6]{0:T(128)S(1)}, s32[6]{0:T(128)}, u32[]{:S(2)}) copy-start(s32[6]{0:T(128)} %blk_ref.1) | copy-start | bytes 76
  22.9 0.7 %copy-start.8 = (s32[64]{0:T(128)S(1)}, s32[64]{0:T(128)}, u32[]{:S(2)}) copy-start(s32[64]{0:T(128)} %len_ref.1) | copy-start | bytes 772
  23.5 14.5 %copy-start = (bf16[1024,4096]{1,0:T(8,128)(2,1)S(1)}, bf16[1024,4096]{1,0:T(8,128)(2,1)}, u32[]{:S(2)}) copy-start(bf16[1024,4096]{1,0:T(8,128)(2,1)} %w_ref.1) | copy-start | bytes 25165828
  23.5 14.5 %copy-start.3 = (bf16[4,1024]{1,0:T(4,128)(2,1)S(1)}, bf16[4,1024]{1,0:T(4,128)(2,1)}, u32[]{:S(2)}) copy-start(bf16[4,1024]{1,0:T(4,128)(2,1)} %q_ref.1) | copy-start | bytes 24580
  23.5 14.5 %copy-start.4 = (bf16[4,128]{1,0:T(4,128)(2,1)S(1)}, bf16[4,128]{1,0:T(4,128)(2,1)}, u32[]{:S(2)}) copy-start(bf16[4,128]{1,0:T(4,128)(2,1)} %key_ref.1) | copy-start | bytes 3076
  23.5 14.5 %copy-start.5 = (bf16[4,128]{1,0:T(4,128)(2,1)S(1)}, bf16[4,128]{1,0:T(4,128)(2,1)}, u32[]{:S(2)}) copy-start(bf16[4,128]{1,0:T(4,128)(2,1)} %value_ref.1) | copy-start | bytes 3076

commit v2 on v1

--- a/solution.py
+++ b/solution.py
@@ -21,20 +21,38 @@
     return row, lane
 
 
-def partials_kernel(req_ref, blk_ref, len_ref, q_ref, k_ref, v_ref, out_ref, rows, sums, stats):
+def partials_kernel(
+    req_hbm, blk_hbm, len_hbm, q_ref, k_hbm, v_hbm, out_ref,
+    req, blk, lens, k_ref, v_ref, rows, sums, stats, scalar_sem, k_sem, v_sem,
+):
     homes, per_home, width = q_ref.shape
     slots, tokens, _ = k_ref.shape
+    scalars = [
+        pltpu.make_async_copy(src, dst, scalar_sem.at[i])
+        for i, (src, dst) in enumerate(((req_hbm, req), (blk_hbm, blk), (len_hbm, lens)))
+    ]
+    key_blocks = [
+        pltpu.make_async_copy(k_hbm.at[s], k_ref.at[s], k_sem.at[s]) for s in range(slots)
+    ]
+    value_blocks = [
+        pltpu.make_async_copy(v_hbm.at[s], v_ref.at[s], v_sem.at[s]) for s in range(slots)
+    ]
+    for copy in scalars + key_blocks + value_blocks:
+        copy.start()
     for i in range(homes):
         rows[per_home * i : per_home * (i + 1), :] = q_ref[i].astype(jnp.float32)
     sums[...] = jnp.zeros_like(sums)
     stats[...] = jnp.full_like(stats, LOW)
     token = lax.broadcasted_iota(jnp.int32, (HEADS, tokens), 1)
-    reqs, peaks, totals, accs = [], [], [], []
-    for s in range(slots):
-        r = req_ref[s]
-        filled = jnp.clip(len_ref[r] - tokens * blk_ref[s], 0, tokens)
+    reqs, peaks, totals, probs, accs = [], [], [], [], []
+    for copy in scalars:
+        copy.wait()
+    for s in range(slots):
+        r = req[s]
+        filled = jnp.clip(lens[r] - tokens * blk[s], 0, tokens)
         row = rows[pl.ds(r, 1), :]
         q = jnp.concatenate([row[:, HEAD * h : HEAD * (h + 1)] for h in range(HEADS)], axis=0)
+        key_blocks[s].wait()
         score = lax.dot_general(
             q.astype(jnp.bfloat16), k_ref[s], (((1,), (1,)), ((), ())),
             preferred_element_type=jnp.float32,
@@ -44,11 +62,14 @@
         peak = jnp.max(score, axis=1, keepdims=True)
         prob = jnp.where(usable, jnp.exp(score - peak), 0.0).astype(jnp.bfloat16)
         total = jnp.sum(prob.astype(jnp.float32), axis=1, keepdims=True)
-        acc = jnp.dot(prob, v_ref[s], preferred_element_type=jnp.float32)
         reqs.append(r)
+        probs.append(prob)
         peaks.append(jnp.broadcast_to(peak, (HEADS, HEAD)))
         totals.append(jnp.broadcast_to(total, (HEADS, HEAD)))
-        accs.append(acc)
+    for copy in value_blocks:
+        copy.wait()
+    for s in range(slots):
+        accs.append(jnp.dot(probs[s], v_ref[s], preferred_element_type=jnp.float32))
     tops = []
     for s in range(slots):
         top = peaks[s]
@@ -130,12 +151,21 @@
     return pl.BlockSpec(memory_space=pltpu.VMEM)
 
 
+def in_hbm(array):
+    return pltpu.with_memory_space_constraint(array, pltpu.HBM)
+
+
+def hbm():
+    return pl.BlockSpec(memory_space=pltpu.HBM)
+
+
 def per_device(
     homes, parts, queries, incoming_keys, incoming_values, cache_keys, pooled_values,
     lengths, slot_request, slot_block, out_weight,
 ):
     mine, width = queries.shape
     cells = mine * HEADS
+    slots = cache_keys.shape[0]
     with jax.named_scope("queries_to_owners"):
         query_all = lax.all_to_all(
             jnp.broadcast_to(queries[None], (homes, mine, width)), "group", 0, 0, tiled=True
@@ -144,15 +174,23 @@
         sent = pl.pallas_call(
             partials_kernel,
             out_shape=jax.ShapeDtypeStruct((homes, cells + STAT_ROWS, HEAD), jnp.bfloat16),
-            in_specs=[pl.BlockSpec(memory_space=pltpu.SMEM)] * 3 + [whole()] * 3,
+            in_specs=[hbm()] * 3 + [whole()] + [hbm()] * 2,
             out_specs=whole(),
             scratch_shapes=[
+                pltpu.SMEM(slot_request.shape, jnp.int32),
+                pltpu.SMEM(slot_block.shape, jnp.int32),
+                pltpu.SMEM(lengths.shape, jnp.int32),
+                pltpu.VMEM(cache_keys.shape, cache_keys.dtype),
+                pltpu.VMEM(pooled_values.shape, pooled_values.dtype),
                 pltpu.VMEM((homes * mine, width), jnp.float32),
                 pltpu.VMEM((homes * mine, HEADS, HEAD), jnp.float32),
                 pltpu.VMEM((homes * mine, HEADS, HEAD), jnp.float32),
+                pltpu.SemaphoreType.DMA((3,)),
+                pltpu.SemaphoreType.DMA((slots,)),
+                pltpu.SemaphoreType.DMA((slots,)),
             ],
             compiler_params=pltpu.CompilerParams(vmem_limit_bytes=24 * MIB),
-        )(slot_request, slot_block, lengths, query_all, cache_keys, pooled_values)
+        )(*(in_hbm(a) for a in (slot_request, slot_block, lengths)), query_all, in_hbm(cache_keys), in_hbm(pooled_values))
     with jax.named_scope("partials_to_homes"):
         got = lax.all_to_all(sent, "group", 0, 0, tiled=True)
     with jax.named_scope("combine_and_project"):

time: 52.4 us -> 46.6 us (0.89)
  local copies, waits for them, and re-layouts: 8.28 us -> 0.75 us
  Pallas kernels: 5.74 us -> 7.58 us
    unnamed x18 -> x8, local copies, waits for them, and re-layouts: 7.55 us -> 0.01 us
    pallas_call x1, Pallas kernels: 4.31 us -> 6.15 us  [per_device(): pl.pallas_call(partials_kernel, out_shape=jax.ShapeDtypeStruct((homes, ce...]
where the time goes in v2:
time: 46.6 us; the launch traced here: 46.3 us
  blocking collectives  37.4 us (80%)
  Pallas kernels  7.58 us (16%)
  local copies, waits for them, and re-layouts  0.75 us (2%)
  other arithmetic  0.62 us (1%)
    all_to_all x1, blocking collectives, per_device(): lax.all_to_all(jnp.broadcast_to(queries[None], (homes, mine, width)), 'gr...  15.3 us
    all_to_all x1, blocking collectives, per_device(): shares = lax.all_to_all(shares, 'tp', 0, 0, tiled=True)  11.9 us
    all_to_all x1, blocking collectives, per_device(): got = lax.all_to_all(sent, 'group', 0, 0, tiled=True)  10.1 us
    pallas_call x1, Pallas kernels, per_device(): pl.pallas_call(partials_kernel, out_shape=jax.ShapeDtypeStruct((homes, ce...  6.15 us
    pallas_call x1, Pallas kernels, per_device(): pl.pallas_call(combine_kernel, out_shape=jax.ShapeDtypeStruct((parts, min...  1.43 us

profile of v2, /device:TPU:1, one launch (start us, length us, event | category | flops | bytes accessed | tf_op | source)
XLA Modules:
  0.0 46.3 jit_solution(8007732882481845013)
XLA Ops:
  0.0 0.7 %broadcast_in_dim.2 = bf16[16,4,1024]{2,1,0:T(4,128)(2,1)S(1)} broadcast(bf16[4,1024]{1,0:T(4,128)(2,1)} %q_ref.1), dimensions={1,2} | broadcast | bytes 139264 | tf_op jit(solution)/shard_map/queries_to_owners/broadcast_in_dim | solution.py:171
  0.7 15.3 %all_to_all.15.q_ref = bf16[16,4,1024]{2,1,0:T(4,128)(2,1)S(1)} all-to-all(bf16[16,4,1024]{2,1,0:T(4,128)(2,1)S(1)} %broadcast_in_dim.2), channel_id=1, replica_groups=mesh['group'=16,'tp'=8] {'group'}, dimensions={0} | all-to-all | bytes 262144 | tf_op jit(solution)/shard_map/queries_to_owners/all_to_all | solution.py:170
  16.0 0.0 copy-start
  16.0 0.0 copy-start.1
  16.0 0.0 copy-start.2
  16.0 0.0 copy-start.3
  16.0 6.2 %slot_partials.1 = bf16[16,40,128]{2,1,0:T(8,128)(2,1)S(1)} custom-call(s32[6]{0:T(128)} %req_hbm.1, s32[6]{0:T(128)} %blk_hbm.1, s32[64]{0:T(128)} %len_hbm.1, bf16[16,4,1024]{2,1,0:T(4,128)(2,1)S(1)} %all_to_all.15.q_ref, bf16[6,4096,128]{2,1,0:T(8,128)(2,1)} %k_hbm.1, bf16[6,4096,128]{2,1,0:T(8,128)(2,1)} %v_hbm.1), custom_call_target="tpu_custom_call" | custom-call | tf_op jit(solution)/shard_map/slot_partials/pallas_call | solution.py:174
  22.2 10.1 %all_to_all.16.got_ref = bf16[16,40,128]{2,1,0:T(8,128)(2,1)S(1)} all-to-all(bf16[16,40,128]{2,1,0:T(8,128)(2,1)S(1)} %slot_partials.1), channel_id=1, replica_groups=mesh['group'=16,'tp'=8] {'group'}, dimensions={0} | all-to-all | bytes 327680 | tf_op jit(solution)/shard_map/partials_to_homes/all_to_all | solution.py:195
  32.3 0.0 copy-done
  32.3 0.0 copy-done.1
  32.3 0.0 copy-done.2
  32.3 0.0 copy-done.3
  32.3 1.4 %combine_and_project.1 = bf16[8,4,512]{2,1,0:T(4,128)(2,1)S(1)} custom-call(bf16[16,40,128]{2,1,0:T(8,128)(2,1)S(1)} %all_to_all.16.got_ref, bf16[4,1024]{1,0:T(4,128)(2,1)S(1)} %copy-done.1, bf16[4,128]{1,0:T(4,128)(2,1)S(1)} %copy-done.2, bf16[4,128]{1,0:T(4,128)(2,1)S(1)} %copy-done.3, bf16[1024,4096]{1,0:T(8,128)(2,1)S(1)} %copy-done), custom_call_target="tpu_custom_call" | custom-call | tf_op jit(solution)/shard_map/combine_and_project/pallas_call | solution.py:197
  33.8 11.9 %all_to_all.17 = bf16[8,4,512]{2,1,0:T(4,128)(2,1)S(1)} all-to-all(bf16[8,4,512]{2,1,0:T(4,128)(2,1)S(1)} %combine_and_project.1), channel_id=1, replica_groups=mesh['group'=16,'tp'=8] {'tp'}, dimensions={0} | all-to-all | bytes 65536 | tf_op jit(solution)/shard_map/sum_over_features/all_to_all | solution.py:208
  45.7 0.6 %reduce_sum.12 = bf16[4,512]{1,0:T(4,128)(2,1)} reduce(bf16[8,4,512]{2,1,0:T(4,128)(2,1)S(1)} %all_to_all.17, bf16[]{:T(256)} %constant.2.clone.1), dimensions={0}, to_apply=%region_0.0 | reduce | flops 14336 | bytes 36866 | tf_op jit(solution)/shard_map/sum_over_features/reduce_sum | solution.py:209
Async XLA Ops:
  16.0 16.3 %copy-start = (bf16[1024,4096]{1,0:T(8,128)(2,1)S(1)}, bf16[1024,4096]{1,0:T(8,128)(2,1)}, u32[]{:S(2)}) copy-start(bf16[1024,4096]{1,0:T(8,128)(2,1)} %w_ref.1) | copy-start | bytes 25165828
  16.0 16.3 %copy-start.1 = (bf16[4,1024]{1,0:T(4,128)(2,1)S(1)}, bf16[4,1024]{1,0:T(4,128)(2,1)}, u32[]{:S(2)}) copy-start(bf16[4,1024]{1,0:T(4,128)(2,1)} %q_ref.1) | copy-start | bytes 24580
  16.0 16.3 %copy-start.2 = (bf16[4,128]{1,0:T(4,128)(2,1)S(1)}, bf16[4,128]{1,0:T(4,128)(2,1)}, u32[]{:S(2)}) copy-start(bf16[4,128]{1,0:T(4,128)(2,1)} %key_ref.1) | copy-start | bytes 3076
  16.0 16.3 %copy-start.3 = (bf16[4,128]{1,0:T(4,128)(2,1)S(1)}, bf16[4,128]{1,0:T(4,128)(2,1)}, u32[]{:S(2)}) copy-start(bf16[4,128]{1,0:T(4,128)(2,1)} %value_ref.1) | copy-start | bytes 3076

commit v3 on v1

--- a/solution.py
+++ b/solution.py
@@ -19,6 +19,10 @@
     row = lax.broadcasted_iota(jnp.int32, shape, len(shape) - 2)
     lane = lax.broadcasted_iota(jnp.int32, shape, len(shape) - 1)
     return row, lane
+
+
+def spread_kernel(q_ref, k_hbm, v_hbm, w_hbm, out_ref):
+    out_ref[...] = jnp.broadcast_to(q_ref[...][None], out_ref.shape)
 
 
 def partials_kernel(req_ref, blk_ref, len_ref, q_ref, k_ref, v_ref, out_ref, rows, sums, stats):
@@ -44,11 +48,10 @@
         peak = jnp.max(score, axis=1, keepdims=True)
         prob = jnp.where(usable, jnp.exp(score - peak), 0.0).astype(jnp.bfloat16)
         total = jnp.sum(prob.astype(jnp.float32), axis=1, keepdims=True)
-        acc = jnp.dot(prob, v_ref[s], preferred_element_type=jnp.float32)
         reqs.append(r)
         peaks.append(jnp.broadcast_to(peak, (HEADS, HEAD)))
         totals.append(jnp.broadcast_to(total, (HEADS, HEAD)))
-        accs.append(acc)
+        accs.append(jnp.dot(prob, v_ref[s], preferred_element_type=jnp.float32))
     tops = []
     for s in range(slots):
         top = peaks[s]
@@ -130,21 +133,39 @@
     return pl.BlockSpec(memory_space=pltpu.VMEM)
 
 
+def in_hbm(array):
+    return pltpu.with_memory_space_constraint(array, pltpu.HBM)
+
+
+def hbm():
+    return pl.BlockSpec(memory_space=pltpu.HBM)
+
+
+def smem():
+    return pl.BlockSpec(memory_space=pltpu.SMEM)
+
+
 def per_device(
     homes, parts, queries, incoming_keys, incoming_values, cache_keys, pooled_values,
     lengths, slot_request, slot_block, out_weight,
 ):
     mine, width = queries.shape
     cells = mine * HEADS
+    slots = cache_keys.shape[0]
     with jax.named_scope("queries_to_owners"):
-        query_all = lax.all_to_all(
-            jnp.broadcast_to(queries[None], (homes, mine, width)), "group", 0, 0, tiled=True
-        )
+        copies = pl.pallas_call(
+            spread_kernel,
+            out_shape=jax.ShapeDtypeStruct((homes, mine, width), queries.dtype),
+            in_specs=[whole()] + [hbm()] * 3,
+            out_specs=whole(),
+            compiler_params=pltpu.CompilerParams(vmem_limit_bytes=4 * MIB),
+        )(queries, in_hbm(cache_keys), in_hbm(pooled_values), in_hbm(out_weight))
+        query_all = lax.all_to_all(copies, "group", 0, 0, tiled=True)
     with jax.named_scope("slot_partials"):
         sent = pl.pallas_call(
             partials_kernel,
             out_shape=jax.ShapeDtypeStruct((homes, cells + STAT_ROWS, HEAD), jnp.bfloat16),
-            in_specs=[pl.BlockSpec(memory_space=pltpu.SMEM)] * 3 + [whole()] * 3,
+            in_specs=[smem()] * 3 + [whole()] * 3,
             out_specs=whole(),
             scratch_shapes=[
                 pltpu.VMEM((homes * mine, width), jnp.float32),

time: 52.4 us -> 45.2 us (0.86)
  local copies, waits for them, and re-layouts: 8.28 us -> 0.89 us
    unnamed x18 -> x20, local copies, waits for them, and re-layouts: 7.55 us -> 0.89 us
    broadcast_in_dim x1 -> x0, local copies, waits for them, and re-layouts: 0.73 us -> none  [per_device(): jnp.broadcast_to(queries[None], (homes, mine, width))]
where the time goes in v3:
time: 45.2 us; the launch traced here: 44.9 us
  blocking collectives  37.6 us (83%)
  Pallas kernels  5.74 us (13%)
  local copies, waits for them, and re-layouts  0.89 us (2%)
  other arithmetic  0.62 us (1%)
    all_to_all x1, blocking collectives, per_device(): query_all = lax.all_to_all(copies, 'group', 0, 0, tiled=True)  15.5 us
    all_to_all x1, blocking collectives, per_device(): shares = lax.all_to_all(shares, 'tp', 0, 0, tiled=True)  11.9 us
    all_to_all x1, blocking collectives, per_device(): got = lax.all_to_all(sent, 'group', 0, 0, tiled=True)  10.1 us
    pallas_call x1, Pallas kernels, per_device(): pl.pallas_call(partials_kernel, out_shape=jax.ShapeDtypeStruct((homes, ce...  4.3 us
    pallas_call x1, Pallas kernels, per_device(): pl.pallas_call(combine_kernel, out_shape=jax.ShapeDtypeStruct((parts, min...  1.43 us

profile of v3, /device:TPU:1, one launch (start us, length us, event | category | flops | bytes accessed | tf_op | source)
XLA Modules:
  0.0 44.9 jit_solution(12332067701742924414)
XLA Ops:
  0.0 0.0 copy-start.2
  0.0 0.0 copy-start.1
  0.0 0.0 copy-start.3
  0.0 0.8 %copy-done.3 = bf16[4,1024]{1,0:T(4,128)(2,1)S(1)} copy-done((bf16[4,1024]{1,0:T(4,128)(2,1)S(1)}, bf16[4,1024]{1,0:T(4,128)(2,1)}, u32[]{:S(2)}) %copy-start.3) | copy-done | bytes 8216
  0.9 0.0 copy-start.7
  0.9 15.5 %all_to_all.15.q_ref = bf16[16,4,1024]{2,1,0:T(4,128)(2,1)S(1)} all-to-all(bf16[16,4,1024]{2,1,0:T(4,128)(2,1)S(1)} %queries_to_owners.1), channel_id=1, replica_groups=mesh['group'=16,'tp'=8] {'group'}, dimensions={0} | all-to-all | bytes 262144 | tf_op jit(solution)/shard_map/queries_to_owners/all_to_all | solution.py:163
  16.4 0.0 copy-done.2
  16.4 0.0 copy-done.1
  16.4 0.0 copy-done.7
  16.4 0.0 copy-done.8
  16.4 0.0 copy-done.9
  16.4 0.0 copy-start
  16.4 0.0 copy-start.4
  16.5 0.0 copy-start.5
  16.5 0.0 copy-start.6
  16.5 4.3 %slot_partials.1 = bf16[16,40,128]{2,1,0:T(8,128)(2,1)S(1)} custom-call(s32[6]{0:T(128)S(1)} %copy-done.7, s32[6]{0:T(128)S(1)} %copy-done.8, s32[64]{0:T(128)S(1)} %copy-done.9, bf16[16,4,1024]{2,1,0:T(4,128)(2,1)S(1)} %all_to_all.15.q_ref, bf16[6,4096,128]{2,1,0:T(8,128)(2,1)S(1)} %copy-done.1, bf16[6,4096,128]{2,1,0:T(8,128)(2,1)S(1)} %copy-done.2), custom_call_target="tpu_custom_call" | custom-call | tf_op jit(solution)/shard_map/slot_partials/pallas_call | solution.py:165
  20.8 10.1 %all_to_all.16.got_ref = bf16[16,40,128]{2,1,0:T(8,128)(2,1)S(1)} all-to-all(bf16[16,40,128]{2,1,0:T(8,128)(2,1)S(1)} %slot_partials.1), channel_id=1, replica_groups=mesh['group'=16,'tp'=8] {'group'}, dimensions={0} | all-to-all | bytes 327680 | tf_op jit(solution)/shard_map/partials_to_homes/all_to_all | solution.py:178
  30.9 0.0 copy-done
  30.9 0.0 copy-done.4
  30.9 0.0 copy-done.5
  30.9 0.0 copy-done.6
  31.0 1.4 %combine_and_project.1 = bf16[8,4,512]{2,1,0:T(4,128)(2,1)S(1)} custom-call(bf16[16,40,128]{2,1,0:T(8,128)(2,1)S(1)} %all_to_all.16.got_ref, bf16[4,1024]{1,0:T(4,128)(2,1)S(1)} %copy-done.4, bf16[4,128]{1,0:T(4,128)(2,1)S(1)} %copy-done.5, bf16[4,128]{1,0:T(4,128)(2,1)S(1)} %copy-done.6, bf16[1024,4096]{1,0:T(8,128)(2,1)S(1)} %copy-done), custom_call_target="tpu_custom_call" | custom-call | tf_op jit(solution)/shard_map/combine_and_project/pallas_call | solution.py:180
  32.4 11.9 %all_to_all.17 = bf16[8,4,512]{2,1,0:T(4,128)(2,1)S(1)} all-to-all(bf16[8,4,512]{2,1,0:T(4,128)(2,1)S(1)} %combine_and_project.1), channel_id=1, replica_groups=mesh['group'=16,'tp'=8] {'tp'}, dimensions={0} | all-to-all | bytes 65536 | tf_op jit(solution)/shard_map/sum_over_features/all_to_all | solution.py:191
  44.3 0.6 %reduce_sum.12 = bf16[4,512]{1,0:T(4,128)(2,1)} reduce(bf16[8,4,512]{2,1,0:T(4,128)(2,1)S(1)} %all_to_all.17, bf16[]{:T(256)} %constant.2.clone.1), dimensions={0}, to_apply=%region_0.0 | reduce | flops 14336 | bytes 36866 | tf_op jit(solution)/shard_map/sum_over_features/reduce_sum | solution.py:192
  (3 shorter events, 0.0 us)
Async XLA Ops:
  0.0 16.4 %copy-start.2 = (bf16[6,4096,128]{2,1,0:T(8,128)(2,1)S(1)}, bf16[6,4096,128]{2,1,0:T(8,128)(2,1)}, u32[]{:S(2)}) copy-start(bf16[6,4096,128]{2,1,0:T(8,128)(2,1)} %v_ref.1) | copy-start | bytes 18874372
  0.0 16.4 %copy-start.1 = (bf16[6,4096,128]{2,1,0:T(8,128)(2,1)S(1)}, bf16[6,4096,128]{2,1,0:T(8,128)(2,1)}, u32[]{:S(2)}) copy-start(bf16[6,4096,128]{2,1,0:T(8,128)(2,1)} %k_ref.1) | copy-start | bytes 18874372
  0.0 0.8 %copy-start.3 = (bf16[4,1024]{1,0:T(4,128)(2,1)S(1)}, bf16[4,1024]{1,0:T(4,128)(2,1)}, u32[]{:S(2)}) copy-start(bf16[4,1024]{1,0:T(4,128)(2,1)} %q_ref.3) | copy-start | bytes 24580
  0.9 15.6 %copy-start.7 = (s32[6]{0:T(128)S(1)}, s32[6]{0:T(128)}, u32[]{:S(2)}) copy-start(s32[6]{0:T(128)} %req_ref.1) | copy-start | bytes 76
  0.9 15.6 %copy-start.8 = (s32[6]{0:T(128)S(1)}, s32[6]{0:T(128)}, u32[]{:S(2)}) copy-start(s32[6]{0:T(128)} %blk_ref.1) | copy-start | bytes 76
  0.9 15.6 %copy-start.9 = (s32[64]{0:T(128)S(1)}, s32[64]{0:T(128)}, u32[]{:S(2)}) copy-start(s32[64]{0:T(128)} %len_ref.1) | copy-start | bytes 772
  16.4 14.5 %copy-start = (bf16[1024,4096]{1,0:T(8,128)(2,1)S(1)}, bf16[1024,4096]{1,0:T(8,128)(2,1)}, u32[]{:S(2)}) copy-start(bf16[1024,4096]{1,0:T(8,128)(2,1)} %w_ref.1) | copy-start | bytes 25165828
  16.4 14.5 %copy-start.4 = (bf16[4,1024]{1,0:T(4,128)(2,1)S(1)}, bf16[4,1024]{1,0:T(4,128)(2,1)}, u32[]{:S(2)}) copy-start(bf16[4,1024]{1,0:T(4,128)(2,1)} %q_ref.3) | copy-start | bytes 24580
  16.5 14.5 %copy-start.5 = (bf16[4,128]{1,0:T(4,128)(2,1)S(1)}, bf16[4,128]{1,0:T(4,128)(2,1)}, u32[]{:S(2)}) copy-start(bf16[4,128]{1,0:T(4,128)(2,1)} %key_ref.1) | copy-start | bytes 3076
  16.5 14.5 %copy-start.6 = (bf16[4,128]{1,0:T(4,128)(2,1)S(1)}, bf16[4,128]{1,0:T(4,128)(2,1)}, u32[]{:S(2)}) copy-start(bf16[4,128]{1,0:T(4,128)(2,1)} %value_ref.1) | copy-start | bytes 3076

commit v4 on v3

--- a/solution.py
+++ b/solution.py
@@ -33,25 +33,31 @@
     sums[...] = jnp.zeros_like(sums)
     stats[...] = jnp.full_like(stats, LOW)
     token = lax.broadcasted_iota(jnp.int32, (HEADS, tokens), 1)
-    reqs, peaks, totals, accs = [], [], [], []
-    for s in range(slots):
-        r = req_ref[s]
-        filled = jnp.clip(len_ref[r] - tokens * blk_ref[s], 0, tokens)
-        row = rows[pl.ds(r, 1), :]
+    rate = 1.0 / math.sqrt(HEAD)
+    reqs = [req_ref[s] for s in range(slots)]
+    scores = []
+    for s in range(slots):
+        row = rows[pl.ds(reqs[s], 1), :]
         q = jnp.concatenate([row[:, HEAD * h : HEAD * (h + 1)] for h in range(HEADS)], axis=0)
-        score = lax.dot_general(
-            q.astype(jnp.bfloat16), k_ref[s], (((1,), (1,)), ((), ())),
-            preferred_element_type=jnp.float32,
-        ) * (1.0 / math.sqrt(HEAD))
-        usable = token < filled
-        score = jnp.where(usable, score, LOW)
+        scores.append(
+            lax.dot_general(
+                q.astype(jnp.bfloat16), k_ref[s], (((1,), (1,)), ((), ())),
+                preferred_element_type=jnp.float32,
+            )
+        )
+    peaks, totals, probs = [], [], []
+    for s in range(slots):
+        filled = jnp.clip(len_ref[reqs[s]] - tokens * blk_ref[s], 0, tokens)
+        score = jnp.where(token < filled, scores[s], LOW)
         peak = jnp.max(score, axis=1, keepdims=True)
-        prob = jnp.where(usable, jnp.exp(score - peak), 0.0).astype(jnp.bfloat16)
-        total = jnp.sum(prob.astype(jnp.float32), axis=1, keepdims=True)
-        reqs.append(r)
-        peaks.append(jnp.broadcast_to(peak, (HEADS, HEAD)))
+        prob = jnp.exp((score - peak) * rate)
+        total = jnp.sum(prob, axis=1, keepdims=True)
+        peaks.append(jnp.broadcast_to(peak * rate, (HEADS, HEAD)))
         totals.append(jnp.broadcast_to(total, (HEADS, HEAD)))
-        accs.append(jnp.dot(prob, v_ref[s], preferred_element_type=jnp.float32))
+        probs.append(prob.astype(jnp.bfloat16))
+    accs = [
+        jnp.dot(probs[s], v_ref[s], preferred_element_type=jnp.float32) for s in range(slots)
+    ]
     tops = []
     for s in range(slots):
         top = peaks[s]

time: 45.2 us -> 44 us (0.973)
  Pallas kernels: 5.74 us -> 4.63 us
    pallas_call x1, Pallas kernels: 4.3 us -> 3.19 us  [per_device(): pl.pallas_call(partials_kernel, out_shape=jax.ShapeDtypeStruct((homes, ce...]
where the time goes in v4:
time: 44 us; the launch traced here: 43.8 us
  blocking collectives  37.6 us (85%)
  Pallas kernels  4.63 us (11%)
  local copies, waits for them, and re-layouts  0.89 us (2%)
  other arithmetic  0.62 us (1%)
    all_to_all x1, blocking collectives, per_device(): query_all = lax.all_to_all(copies, 'group', 0, 0, tiled=True)  15.5 us
    all_to_all x1, blocking collectives, per_device(): shares = lax.all_to_all(shares, 'tp', 0, 0, tiled=True)  11.9 us
    all_to_all x1, blocking collectives, per_device(): got = lax.all_to_all(sent, 'group', 0, 0, tiled=True)  10.1 us
    pallas_call x1, Pallas kernels, per_device(): pl.pallas_call(partials_kernel, out_shape=jax.ShapeDtypeStruct((homes, ce...  3.19 us
    pallas_call x1, Pallas kernels, per_device(): pl.pallas_call(combine_kernel, out_shape=jax.ShapeDtypeStruct((parts, min...  1.43 us
    unnamed x20, local copies, waits for them, and re-layouts  0.89 us

profile of v4, /device:TPU:1, one launch (start us, length us, event | category | flops | bytes accessed | tf_op | source)
XLA Modules:
  0.0 43.8 jit_solution(11383564256838628565)
XLA Ops:
  0.0 0.0 copy-start.2
  0.0 0.0 copy-start.1
  0.0 0.0 copy-start.3
  0.0 0.8 %copy-done.3 = bf16[4,1024]{1,0:T(4,128)(2,1)S(1)} copy-done((bf16[4,1024]{1,0:T(4,128)(2,1)S(1)}, bf16[4,1024]{1,0:T(4,128)(2,1)}, u32[]{:S(2)}) %copy-start.3) | copy-done | bytes 8216
  0.9 0.0 copy-start.7
  0.9 15.5 %all_to_all.15.q_ref = bf16[16,4,1024]{2,1,0:T(4,128)(2,1)S(1)} all-to-all(bf16[16,4,1024]{2,1,0:T(4,128)(2,1)S(1)} %queries_to_owners.1), channel_id=1, replica_groups=mesh['group'=16,'tp'=8] {'group'}, dimensions={0} | all-to-all | bytes 262144 | tf_op jit(solution)/shard_map/queries_to_owners/all_to_all | solution.py:169
  16.4 0.0 copy-done.2
  16.4 0.0 copy-done.1
  16.4 0.0 copy-done.7
  16.4 0.0 copy-done.8
  16.4 0.0 copy-done.9
  16.4 0.0 copy-start
  16.4 0.0 copy-start.4
  16.5 0.0 copy-start.5
  16.5 0.0 copy-start.6
  16.5 3.2 %slot_partials.1 = bf16[16,40,128]{2,1,0:T(8,128)(2,1)S(1)} custom-call(s32[6]{0:T(128)S(1)} %copy-done.7, s32[6]{0:T(128)S(1)} %copy-done.8, s32[64]{0:T(128)S(1)} %copy-done.9, bf16[16,4,1024]{2,1,0:T(4,128)(2,1)S(1)} %all_to_all.15.q_ref, bf16[6,4096,128]{2,1,0:T(8,128)(2,1)S(1)} %copy-done.1, bf16[6,4096,128]{2,1,0:T(8,128)(2,1)S(1)} %copy-done.2), custom_call_target="tpu_custom_call" | custom-call | tf_op jit(solution)/shard_map/slot_partials/pallas_call | solution.py:171
  19.7 10.1 %all_to_all.16.got_ref = bf16[16,40,128]{2,1,0:T(8,128)(2,1)S(1)} all-to-all(bf16[16,40,128]{2,1,0:T(8,128)(2,1)S(1)} %slot_partials.1), channel_id=1, replica_groups=mesh['group'=16,'tp'=8] {'group'}, dimensions={0} | all-to-all | bytes 327680 | tf_op jit(solution)/shard_map/partials_to_homes/all_to_all | solution.py:184
  29.8 0.0 copy-done
  29.8 0.0 copy-done.4
  29.8 0.0 copy-done.5
  29.8 0.0 copy-done.6
  29.8 1.4 %combine_and_project.1 = bf16[8,4,512]{2,1,0:T(4,128)(2,1)S(1)} custom-call(bf16[16,40,128]{2,1,0:T(8,128)(2,1)S(1)} %all_to_all.16.got_ref, bf16[4,1024]{1,0:T(4,128)(2,1)S(1)} %copy-done.4, bf16[4,128]{1,0:T(4,128)(2,1)S(1)} %copy-done.5, bf16[4,128]{1,0:T(4,128)(2,1)S(1)} %copy-done.6, bf16[1024,4096]{1,0:T(8,128)(2,1)S(1)} %copy-done), custom_call_target="tpu_custom_call" | custom-call | tf_op jit(solution)/shard_map/combine_and_project/pallas_call | solution.py:186
  31.3 11.9 %all_to_all.17 = bf16[8,4,512]{2,1,0:T(4,128)(2,1)S(1)} all-to-all(bf16[8,4,512]{2,1,0:T(4,128)(2,1)S(1)} %combine_and_project.1), channel_id=1, replica_groups=mesh['group'=16,'tp'=8] {'tp'}, dimensions={0} | all-to-all | bytes 65536 | tf_op jit(solution)/shard_map/sum_over_features/all_to_all | solution.py:197
  43.2 0.6 %reduce_sum.12 = bf16[4,512]{1,0:T(4,128)(2,1)} reduce(bf16[8,4,512]{2,1,0:T(4,128)(2,1)S(1)} %all_to_all.17, bf16[]{:T(256)} %constant.2.clone.1), dimensions={0}, to_apply=%region_0.0 | reduce | flops 14336 | bytes 36866 | tf_op jit(solution)/shard_map/sum_over_features/reduce_sum | solution.py:198
  (3 shorter events, 0.0 us)
Async XLA Ops:
  0.0 16.4 %copy-start.2 = (bf16[6,4096,128]{2,1,0:T(8,128)(2,1)S(1)}, bf16[6,4096,128]{2,1,0:T(8,128)(2,1)}, u32[]{:S(2)}) copy-start(bf16[6,4096,128]{2,1,0:T(8,128)(2,1)} %v_ref.1) | copy-start | bytes 18874372
  0.0 16.4 %copy-start.1 = (bf16[6,4096,128]{2,1,0:T(8,128)(2,1)S(1)}, bf16[6,4096,128]{2,1,0:T(8,128)(2,1)}, u32[]{:S(2)}) copy-start(bf16[6,4096,128]{2,1,0:T(8,128)(2,1)} %k_ref.1) | copy-start | bytes 18874372
  0.0 0.8 %copy-start.3 = (bf16[4,1024]{1,0:T(4,128)(2,1)S(1)}, bf16[4,1024]{1,0:T(4,128)(2,1)}, u32[]{:S(2)}) copy-start(bf16[4,1024]{1,0:T(4,128)(2,1)} %q_ref.3) | copy-start | bytes 24580
  0.9 15.6 %copy-start.7 = (s32[6]{0:T(128)S(1)}, s32[6]{0:T(128)}, u32[]{:S(2)}) copy-start(s32[6]{0:T(128)} %req_ref.1) | copy-start | bytes 76
  0.9 15.6 %copy-start.8 = (s32[6]{0:T(128)S(1)}, s32[6]{0:T(128)}, u32[]{:S(2)}) copy-start(s32[6]{0:T(128)} %blk_ref.1) | copy-start | bytes 76
  0.9 15.6 %copy-start.9 = (s32[64]{0:T(128)S(1)}, s32[64]{0:T(128)}, u32[]{:S(2)}) copy-start(s32[64]{0:T(128)} %len_ref.1) | copy-start | bytes 772
  16.4 13.4 %copy-start = (bf16[1024,4096]{1,0:T(8,128)(2,1)S(1)}, bf16[1024,4096]{1,0:T(8,128)(2,1)}, u32[]{:S(2)}) copy-start(bf16[1024,4096]{1,0:T(8,128)(2,1)} %w_ref.1) | copy-start | bytes 25165828
  16.4 13.4 %copy-start.4 = (bf16[4,1024]{1,0:T(4,128)(2,1)S(1)}, bf16[4,1024]{1,0:T(4,128)(2,1)}, u32[]{:S(2)}) copy-start(bf16[4,1024]{1,0:T(4,128)(2,1)} %q_ref.3) | copy-start | bytes 24580
  16.5 13.4 %copy-start.5 = (bf16[4,128]{1,0:T(4,128)(2,1)S(1)}, bf16[4,128]{1,0:T(4,128)(2,1)}, u32[]{:S(2)}) copy-start(bf16[4,128]{1,0:T(4,128)(2,1)} %key_ref.1) | copy-start | bytes 3076
  16.5 13.4 %copy-start.6 = (bf16[4,128]{1,0:T(4,128)(2,1)S(1)}, bf16[4,128]{1,0:T(4,128)(2,1)}, u32[]{:S(2)}) copy-start(bf16[4,128]{1,0:T(4,128)(2,1)} %value_ref.1) | copy-start | bytes 3076

commit v5 on v4

--- a/solution.py
+++ b/solution.py
@@ -21,24 +21,47 @@
     return row, lane
 
 
-def spread_kernel(q_ref, k_hbm, v_hbm, w_hbm, out_ref):
+def spread_kernel(q_ref, out_ref):
     out_ref[...] = jnp.broadcast_to(q_ref[...][None], out_ref.shape)
 
 
-def partials_kernel(req_ref, blk_ref, len_ref, q_ref, k_ref, v_ref, out_ref, rows, sums, stats):
+def pass_kernel(q_ref, k_hbm, v_hbm, w_hbm, out_ref):
+    out_ref[...] = q_ref[...]
+
+
+def columns(row_ref, mask):
+    row = jnp.broadcast_to(row_ref[...].astype(jnp.float32), mask.shape)
+    return jnp.sum(jnp.where(mask, row, 0.0), axis=1, keepdims=True)
+
+
+def partials_kernel(
+    req_ref, blk_ref, len_ref, q_ref, k_ref, v_ref, out_ref, rows, sums, stats, req, req_sem
+):
     homes, per_home, width = q_ref.shape
     slots, tokens, _ = k_ref.shape
+    copy = pltpu.make_async_copy(req_ref, req, req_sem)
+    copy.start()
+    row, lane = same_lane((HEADS, slots))
+    request = columns(req_ref, row == lane)
+    block = columns(blk_ref, row == lane)
+    _, lane = same_lane((HEADS, homes * per_home))
+    chosen = lane.astype(jnp.float32) == request
+    filled = jnp.clip(columns(len_ref, chosen) - tokens * block, 0, tokens).astype(jnp.int32)
     for i in range(homes):
         rows[per_home * i : per_home * (i + 1), :] = q_ref[i].astype(jnp.float32)
     sums[...] = jnp.zeros_like(sums)
     stats[...] = jnp.full_like(stats, LOW)
     token = lax.broadcasted_iota(jnp.int32, (HEADS, tokens), 1)
     rate = 1.0 / math.sqrt(HEAD)
-    reqs = [req_ref[s] for s in range(slots)]
+    gathered = jnp.dot(
+        chosen.astype(jnp.bfloat16), rows[...].astype(jnp.bfloat16),
+        preferred_element_type=jnp.float32,
+    )
     scores = []
     for s in range(slots):
-        row = rows[pl.ds(reqs[s], 1), :]
-        q = jnp.concatenate([row[:, HEAD * h : HEAD * (h + 1)] for h in range(HEADS)], axis=0)
+        q = jnp.concatenate(
+            [gathered[s : s + 1, HEAD * h : HEAD * (h + 1)] for h in range(HEADS)], axis=0
+        )
         scores.append(
             lax.dot_general(
                 q.astype(jnp.bfloat16), k_ref[s], (((1,), (1,)), ((), ())),
@@ -47,8 +70,7 @@
         )
     peaks, totals, probs = [], [], []
     for s in range(slots):
-        filled = jnp.clip(len_ref[reqs[s]] - tokens * blk_ref[s], 0, tokens)
-        score = jnp.where(token < filled, scores[s], LOW)
+        score = jnp.where(token < filled[s : s + 1, :], scores[s], LOW)
         peak = jnp.max(score, axis=1, keepdims=True)
         prob = jnp.exp((score - peak) * rate)
         total = jnp.sum(prob, axis=1, keepdims=True)
@@ -58,25 +80,27 @@
     accs = [
         jnp.dot(probs[s], v_ref[s], preferred_element_type=jnp.float32) for s in range(slots)
     ]
+    names = [jnp.broadcast_to(request[s : s + 1, :], (HEADS, HEAD)) for s in range(slots)]
     tops = []
     for s in range(slots):
         top = peaks[s]
         for o in range(slots):
             if o != s:
-                top = jnp.where(reqs[o] == reqs[s], jnp.maximum(top, peaks[o]), top)
+                top = jnp.where(names[o] == names[s], jnp.maximum(top, peaks[o]), top)
         tops.append(top)
     weights = [jnp.exp(peaks[s] - tops[s]) for s in range(slots)]
     totals = [weights[s] * totals[s] for s in range(slots)]
     accs = [weights[s] * accs[s] for s in range(slots)]
+    copy.wait()
     for s in range(slots):
         total, acc = totals[s], accs[s]
         for o in range(slots):
             if o != s:
-                same = reqs[o] == reqs[s]
+                same = names[o] == names[s]
                 total = total + jnp.where(same, totals[o], 0.0)
                 acc = acc + jnp.where(same, accs[o], 0.0)
-        sums[reqs[s]] = acc / total
-        stats[reqs[s]] = tops[s] + jnp.log(total)
+        sums[req[0, s]] = acc / total
+        stats[req[0, s]] = tops[s] + jnp.log(total)
     cells = per_home * HEADS
     out_ref[:, :cells, :] = sums[...].reshape(homes, cells, HEAD).astype(jnp.bfloat16)
     row, lane = same_lane((homes, cells, HEAD))
@@ -93,7 +117,7 @@
     out_ref[:, cells:, :] = jnp.broadcast_to(coded, (homes, STAT_ROWS, HEAD)).astype(jnp.bfloat16)
 
 
-def combine_kernel(got_ref, q_ref, key_ref, value_ref, w_ref, out_ref, rows):
+def combine_kernel(got_ref, q_ref, key_ref, value_ref, w_ref, out_ref, att_ref, rows):
     homes = got_ref.shape[0]
     mine = q_ref.shape[0]
     cells = mine * HEADS
@@ -128,11 +152,30 @@
     attention = jnp.concatenate(
         [rows[pl.ds(h, mine, stride=HEADS), :] for h in range(HEADS)], axis=1
     ).astype(jnp.bfloat16)
-    parts, _, width = out_ref.shape
-    for p in range(parts):
-        out_ref[p] = jnp.dot(
-            attention, w_ref[:, width * p : width * (p + 1)], preferred_element_type=jnp.float32
+    att_ref[...] = attention
+    project(attention, w_ref, out_ref, 1 - lax.axis_index("tp") % 2)
+
+
+def project(attention, w_ref, out_ref, core):
+    chips, _, width = out_ref.shape
+    for chip in range(chips):
+        first = pl.multiple_of((2 * chip + core) * width, width)
+        out_ref[chip] = jnp.dot(
+            attention, w_ref[:, pl.ds(first, width)], preferred_element_type=jnp.float32
         ).astype(out_ref.dtype)
+
+
+def own_kernel(att_ref, w_ref, out_ref):
+    project(att_ref[...], w_ref, out_ref, lax.axis_index("tp") % 2)
+
+
+def add_kernel(got_ref, mine_ref, own_ref, *sent_refs):
+    chips = got_ref.shape[0]
+    me = lax.axis_index("tp") // 2
+    own_ref[...] = mine_ref[me] + got_ref[me].astype(jnp.float32)
+    for k, ref in enumerate(sent_refs):
+        chip = lax.rem(me + k + 1, chips)
+        ref[...] = (mine_ref[chip] + got_ref[chip].astype(jnp.float32)).astype(ref.dtype)
 
 
 def whole():
@@ -145,10 +188,6 @@
 
 def hbm():
     return pl.BlockSpec(memory_space=pltpu.HBM)
-
-
-def smem():
-    return pl.BlockSpec(memory_space=pltpu.SMEM)
 
 
 def per_device(
@@ -162,40 +201,79 @@
         copies = pl.pallas_call(
             spread_kernel,
             out_shape=jax.ShapeDtypeStruct((homes, mine, width), queries.dtype),
+            in_specs=[whole()],
+            out_specs=whole(),
+            compiler_params=pltpu.CompilerParams(vmem_limit_bytes=4 * MIB),
+        )(queries)
+        copies = pl.pallas_call(
+            pass_kernel,
+            out_shape=jax.ShapeDtypeStruct((homes, mine, width), queries.dtype),
             in_specs=[whole()] + [hbm()] * 3,
             out_specs=whole(),
             compiler_params=pltpu.CompilerParams(vmem_limit_bytes=4 * MIB),
-        )(queries, in_hbm(cache_keys), in_hbm(pooled_values), in_hbm(out_weight))
+        )(copies, in_hbm(cache_keys), in_hbm(pooled_values), in_hbm(out_weight))
         query_all = lax.all_to_all(copies, "group", 0, 0, tiled=True)
     with jax.named_scope("slot_partials"):
         sent = pl.pallas_call(
             partials_kernel,
             out_shape=jax.ShapeDtypeStruct((homes, cells + STAT_ROWS, HEAD), jnp.bfloat16),
-            in_specs=[smem()] * 3 + [whole()] * 3,
+            in_specs=[whole()] * 6,
             out_specs=whole(),
             scratch_shapes=[
                 pltpu.VMEM((homes * mine, width), jnp.float32),
                 pltpu.VMEM((homes * mine, HEADS, HEAD), jnp.float32),
                 pltpu.VMEM((homes * mine, HEADS, HEAD), jnp.float32),
+                pltpu.SMEM((1, slots), jnp.int32),
+                pltpu.SemaphoreType.DMA,
             ],
             compiler_params=pltpu.CompilerParams(vmem_limit_bytes=24 * MIB),
-        )(slot_request, slot_block, lengths, query_all, cache_keys, pooled_values)
+        )(
+            slot_request[None], slot_block[None], lengths[None],
+            query_all, cache_keys, pooled_values,
+        )
     with jax.named_scope("partials_to_homes"):
         got = lax.all_to_all(sent, "group", 0, 0, tiled=True)
+    chips = parts // 2
+    piece = (mine, out_weight.shape[1] // parts)
     with jax.named_scope("combine_and_project"):
-        shares = pl.pallas_call(
+        other, attention = pl.pallas_call(
             combine_kernel,
-            out_shape=jax.ShapeDtypeStruct(
-                (parts, mine, out_weight.shape[1] // parts), jnp.bfloat16
-            ),
+            out_shape=[
+                jax.ShapeDtypeStruct((chips, *piece), jnp.bfloat16),
+                jax.ShapeDtypeStruct((mine, out_weight.shape[0]), jnp.bfloat16),
+            ],
             in_specs=[whole()] * 5,
-            out_specs=whole(),
+            out_specs=[whole()] * 2,
             scratch_shapes=[pltpu.VMEM((cells, HEAD), jnp.float32)],
             compiler_params=pltpu.CompilerParams(vmem_limit_bytes=16 * MIB),
         )(got, queries, incoming_keys, incoming_values, out_weight)
-    with jax.named_scope("sum_over_features"):
-        shares = lax.all_to_all(shares, "tp", 0, 0, tiled=True)
-        return jnp.sum(shares.astype(jnp.float32), axis=0).astype(jnp.bfloat16)
+    with jax.named_scope("swap_cores"):
+        swapped = lax.ppermute(other, "tp", [(i, i ^ 1) for i in range(parts)])
+    with jax.named_scope("project_own"):
+        own = pl.pallas_call(
+            own_kernel,
+            out_shape=jax.ShapeDtypeStruct((chips, *piece), jnp.float32),
+            in_specs=[whole()] * 2,
+            out_specs=whole(),
+            cost_estimate=pl.CostEstimate(
+                flops=0, bytes_accessed=out_weight.size, transcendentals=0
+            ),
+            compiler_params=pltpu.CompilerParams(vmem_limit_bytes=16 * MIB),
+        )(attention, out_weight)
+    with jax.named_scope("add_cores"):
+        total, *sent = pl.pallas_call(
+            add_kernel,
+            out_shape=[jax.ShapeDtypeStruct(piece, jnp.float32)]
+            + [jax.ShapeDtypeStruct(piece, jnp.bfloat16)] * (chips - 1),
+            in_specs=[whole()] * 2,
+            out_specs=[whole()] * chips,
+            compiler_params=pltpu.CompilerParams(vmem_limit_bytes=4 * MIB),
+        )(swapped, own)
+    with jax.named_scope("sum_over_chips"):
+        for k, array in enumerate(sent):
+            moves = [(i, (i + 2 * (k + 1)) % parts) for i in range(parts)]
+            total = total + lax.ppermute(array, "tp", moves).astype(jnp.float32)
+        return total.astype(jnp.bfloat16)
 
 
 def solution(mesh):

time: 44 us -> 42 us (0.955)
  blocking collectives: 37.6 us -> 25.7 us
  starting transfers between devices: 0 us -> 8.03 us
  waiting for transfers between devices: 0 us -> 1.78 us
    all_to_all x1 -> x0, blocking collectives: 11.9 us -> none  [per_device(): shares = lax.all_to_all(shares, 'tp', 0, 0, tiled=True)]
    ppermute x0 -> x4, starting transfers between devices: none -> 8.03 us  [the longest x3 4.89 us: per_device(): total = total + lax.ppermute(array, 'tp', moves).astype(jnp.float32)]
    ppermute x0 -> x4, waiting for transfers between devices: none -> 1.78 us  [the longest x3 1.6 us: per_device(): total = total + lax.ppermute(array, 'tp', moves).astype(jnp.float32)]
    reduce_sum x1 -> x0, other arithmetic: 0.62 us -> none  [per_device(): return jnp.sum(shares.astype(jnp.float32), axis=0).astype(jnp.bfloat16)]
    convert_element_type x0 -> x1, other arithmetic: none -> 0.6 us  [per_device(): return total.astype(jnp.bfloat16)]
    pallas_call x1 -> x4, Pallas kernels: 1.43 us -> 1.57 us  [the longest x1 0.89 us: per_device(): pl.pallas_call(combine_kernel, out_shape=[jax.ShapeDtypeStruct((chips, *p...]
  transfers between devices with their start and end apart: 0 -> 4, of which waited for: 0 -> 3; matrix products, arithmetic and copies ran while one was open for 0% -> 0% of each run, Pallas kernels for 0% -> 2%
where the time goes in v5:
time: 42 us; the launch traced here: 41.5 us
  blocking collectives  25.7 us (61%)
  starting transfers between devices  8.03 us (19%)
  Pallas kernels  4.49 us (11%)
  waiting for transfers between devices  1.78 us (4%)
  local copies, waits for them, and re-layouts  0.75 us (2%)
  other arithmetic  0.6 us (1%)
    all_to_all x1, blocking collectives, per_device(): query_all = lax.all_to_all(copies, 'group', 0, 0, tiled=True)  15.5 us
    all_to_all x1, blocking collectives, per_device(): got = lax.all_to_all(sent, 'group', 0, 0, tiled=True)  10.1 us
    ppermute x3, starting transfers between devices, per_device(): total = total + lax.ppermute(array, 'tp', moves).astype(jnp.float32)  4.89 us
    ppermute x1, starting transfers between devices, per_device(): swapped = lax.ppermute(other, 'tp', [(i, i ^ 1) for i in range(parts)])  3.14 us
    pallas_call x1, Pallas kernels, per_device(): pl.pallas_call(partials_kernel, out_shape=jax.ShapeDtypeStruct((homes, ce...  2.91 us
    ppermute x3, waiting for transfers between devices, per_device(): total = total + lax.ppermute(array, 'tp', moves).astype(jnp.float32)  1.6 us
    pallas_call x1, Pallas kernels, per_device(): pl.pallas_call(combine_kernel, out_shape=[jax.ShapeDtypeStruct((chips, *p...  0.89 us
  transfers between devices with their start and end apart: 4, of which 3 were waited for; matrix products, arithmetic and copies ran while one was open for 0% of the time, Pallas kernels for 2%

profile of v5, /device:TPU:1, one launch (start us, length us, event | category | flops | bytes accessed | tf_op | source)
XLA Modules:
  0.0 41.5 jit_solution(14581199802446400136)
XLA Ops:
  0.0 0.7 %copy-done.3 = bf16[4,1024]{1,0:T(4,128)(2,1)S(1)} copy-done((bf16[4,1024]{1,0:T(4,128)(2,1)S(1)}, bf16[4,1024]{1,0:T(4,128)(2,1)}, u32[]{:S(2)}) %copy-start.3) | copy-done | bytes 8216
  0.7 0.0 copy-start.1
  0.7 0.0 copy-start.2
  0.7 0.0 copy-start.7
  0.7 0.0 copy-start.8
  0.8 0.0 copy-start.9
  0.8 15.5 %all_to_all.10.q_ref = bf16[16,4,1024]{2,1,0:T(4,128)(2,1)S(1)} all-to-all(bf16[16,4,1024]{2,1,0:T(4,128)(2,1)S(1)} %queries_to_owners.3), channel_id=1, replica_groups=mesh['group'=16,'tp'=8] {'group'}, dimensions={0} | all-to-all | bytes 262144 | tf_op jit(solution)/shard_map/queries_to_owners/all_to_all | solution.py:215
  16.3 0.0 copy-start
  16.4 0.0 copy-start.4
  16.4 0.0 copy-start.5
  16.4 0.0 copy-start.6
  16.4 2.9 %slot_partials.1 = bf16[16,40,128]{2,1,0:T(8,128)(2,1)S(1)} custom-call(s32[1,6]{1,0:T(1,128)S(1)} %bitcast.3, s32[1,6]{1,0:T(1,128)S(1)} %bitcast.4, s32[1,64]{1,0:T(1,128)S(1)} %bitcast.5, bf16[16,4,1024]{2,1,0:T(4,128)(2,1)S(1)} %all_to_all.10.q_ref, bf16[6,4096,128]{2,1,0:T(8,128)(2,1)S(1)} %copy-done.1, bf16[6,4096,128]{2,1,0:T(8,128)(2,1)S(1)} %copy-done.2), custom_call_target="tpu_custom_call" | custom-call | tf_op jit(solution)/shard_map/slot_partials/pallas_call | solution.py:217
  19.3 10.1 %all_to_all.11.got_ref = bf16[16,40,128]{2,1,0:T(8,128)(2,1)S(1)} all-to-all(bf16[16,40,128]{2,1,0:T(8,128)(2,1)S(1)} %slot_partials.1), channel_id=1, replica_groups=mesh['group'=16,'tp'=8] {'group'}, dimensions={0} | all-to-all | bytes 327680 | tf_op jit(solution)/shard_map/partials_to_homes/all_to_all | solution.py:235
  29.5 0.9 %combine_and_project.1 = (bf16[4,4,512]{2,1,0:T(4,128)(2,1)S(1)}, bf16[4,1024]{1,0:T(4,128)(2,1)S(1)}) custom-call(bf16[16,40,128]{2,1,0:T(8,128)(2,1)S(1)} %all_to_all.11.got_ref, bf16[4,1024]{1,0:T(4,128)(2,1)S(1)} %copy-done.4, bf16[4,128]{1,0:T(4,128)(2,1)S(1)} %copy-done.5, bf16[4,128]{1,0:T(4,128)(2,1)S(1)} %copy-done.6, bf16[1024,4096]{1,0:T(8,128)(2,1)S(1)} %copy-done), custom_call_target="tpu_custom_call" | custom-call | tf_op jit(solution)/shard_map/combine_and_project/pallas_call | solution.py:239
  30.4 3.1 %collective-permute-start = (bf16[4,4,512]{2,1,0:T(4,128)(2,1)S(1)}, bf16[4,4,512]{2,1,0:T(4,128)(2,1)S(1)}, u32[]{:S(2)}, u32[]{:S(2)}) collective-permute-start(bf16[4,4,512]{2,1,0:T(4,128)(2,1)S(1)} %get-tuple-element.11), channel_id=1, source_target_pairs={{0,1},{1,0},{2,3},{3,2},{4,5},{5,4},{6,7},{7,6},{8,9},{9,8},{10,11... | collective-permute-start | bytes 49160 | tf_op jit(solution)/shard_map/swap_cores/ppermute | solution.py:251
  33.5 0.7 %project_own.1.mine_ref = f32[4,4,512]{2,1,0:T(4,128)S(1)} custom-call(bf16[4,1024]{1,0:T(4,128)(2,1)S(1)} %get-tuple-element.12.att_ref, bf16[1024,4096]{1,0:T(8,128)(2,1)S(1)} %copy-done), custom_call_target="tpu_custom_call" | custom-call | bytes 4194304 | tf_op jit(solution)/shard_map/project_own/pallas_call | solution.py:253
  34.2 0.2 collective-permute-done.got_ref
  34.4 1.3 %collective-permute-start.1 = (bf16[4,512]{1,0:T(4,128)(2,1)S(1)}, bf16[4,512]{1,0:T(4,128)(2,1)S(1)}, u32[]{:S(2)}, u32[]{:S(2)}) collective-permute-start(bf16[4,512]{1,0:T(4,128)(2,1)S(1)} %get-tuple-element.14), channel_id=1, source_target_pairs={{0,2},{1,3},{2,4},{3,5},{4,6},{5,7},{6,0},{7,1},{8,10},{9,11},{10,... | collective-permute-start | bytes 12296 | tf_op jit(solution)/shard_map/sum_over_chips/ppermute | solution.py:275
  35.6 2.5 %collective-permute-start.2 = (bf16[4,512]{1,0:T(4,128)(2,1)S(1)}, bf16[4,512]{1,0:T(4,128)(2,1)S(1)}, u32[]{:S(2)}, u32[]{:S(2)}) collective-permute-start(bf16[4,512]{1,0:T(4,128)(2,1)S(1)} %get-tuple-element.15), channel_id=1, source_target_pairs={{0,4},{1,5},{2,6},{3,7},{4,0},{5,1},{6,2},{7,3},{8,12},{9,13},{10,... | collective-permute-start | bytes 12296 | tf_op jit(solution)/shard_map/sum_over_chips/ppermute | solution.py:275
  38.1 1.2 %collective-permute-start.3 = (bf16[4,512]{1,0:T(4,128)(2,1)S(1)}, bf16[4,512]{1,0:T(4,128)(2,1)S(1)}, u32[]{:S(2)}, u32[]{:S(2)}) collective-permute-start(bf16[4,512]{1,0:T(4,128)(2,1)S(1)} %get-tuple-element.16), channel_id=1, source_target_pairs={{0,6},{1,7},{2,0},{3,1},{4,2},{5,3},{6,4},{7,5},{8,14},{9,15},{10,... | collective-permute-start | bytes 12296 | tf_op jit(solution)/shard_map/sum_over_chips/ppermute | solution.py:275
  39.3 0.0 collective-permute-done.1
  39.3 0.4 collective-permute-done.2
  39.6 1.2 %collective-permute-done.3 = bf16[4,512]{1,0:T(4,128)(2,1)S(1)} collective-permute-done((bf16[4,512]{1,0:T(4,128)(2,1)S(1)}, bf16[4,512]{1,0:T(4,128)(2,1)S(1)}, u32[]{:S(2)}, u32[]{:S(2)}) %collective-permute-start.3) | collective-permute-done | bytes 4128 | tf_op jit(solution)/shard_map/sum_over_chips/ppermute | solution.py:275
  40.9 0.6 %add_convert_fusion = bf16[4,512]{1,0:T(4,128)(2,1)} fusion(bf16[4,512]{1,0:T(4,128)(2,1)S(1)} %collective-permute-done.3, bf16[4,512]{1,0:T(4,128)(2,1)S(1)} %collective-permute-done.2, f32[4,512]{1,0:T(4,128)S(1)} %get-tuple-element.13, bf16[4,512]{1,0:T(4,128)(2,1)S(1)} %collective-permute-done.1), kind=kLoop, calls=%fused_computation | loop fusion | flops 14336 | bytes 24576 | tf_op jit(solution)/shard_map/sum_over_chips/convert_element_type | solution.py:276
  (13 shorter events, 0.1 us)
Async XLA Ops:
  0.0 0.7 %copy-start.3 = (bf16[4,1024]{1,0:T(4,128)(2,1)S(1)}, bf16[4,1024]{1,0:T(4,128)(2,1)}, u32[]{:S(2)}) copy-start(bf16[4,1024]{1,0:T(4,128)(2,1)} %q_ref.3) | copy-start | bytes 24580
  0.7 15.6 %copy-start.1 = (bf16[6,4096,128]{2,1,0:T(8,128)(2,1)S(1)}, bf16[6,4096,128]{2,1,0:T(8,128)(2,1)}, u32[]{:S(2)}) copy-start(bf16[6,4096,128]{2,1,0:T(8,128)(2,1)} %k_ref.1) | copy-start | bytes 18874372
  0.7 15.6 %copy-start.2 = (bf16[6,4096,128]{2,1,0:T(8,128)(2,1)S(1)}, bf16[6,4096,128]{2,1,0:T(8,128)(2,1)}, u32[]{:S(2)}) copy-start(bf16[6,4096,128]{2,1,0:T(8,128)(2,1)} %v_ref.1) | copy-start | bytes 18874372
  0.7 15.6 %copy-start.7 = (s32[6]{0:T(128)S(1)}, s32[6]{0:T(128)}, u32[]{:S(2)}) copy-start(s32[6]{0:T(128)} %param.15) | copy-start | bytes 76
  0.7 15.6 %copy-start.8 = (s32[6]{0:T(128)S(1)}, s32[6]{0:T(128)}, u32[]{:S(2)}) copy-start(s32[6]{0:T(128)} %param.16) | copy-start | bytes 76
  0.8 15.6 %copy-start.9 = (s32[64]{0:T(128)S(1)}, s32[64]{0:T(128)}, u32[]{:S(2)}) copy-start(s32[64]{0:T(128)} %param.14) | copy-start | bytes 772
  16.3 13.1 %copy-start = (bf16[1024,4096]{1,0:T(8,128)(2,1)S(1)}, bf16[1024,4096]{1,0:T(8,128)(2,1)}, u32[]{:S(2)}) copy-start(bf16[1024,4096]{1,0:T(8,128)(2,1)} %w_ref.3) | copy-start | bytes 25165828
  16.4 13.1 %copy-start.4 = (bf16[4,1024]{1,0:T(4,128)(2,1)S(1)}, bf16[4,1024]{1,0:T(4,128)(2,1)}, u32[]{:S(2)}) copy-start(bf16[4,1024]{1,0:T(4,128)(2,1)} %q_ref.3) | copy-start | bytes 24580
  16.4 13.1 %copy-start.5 = (bf16[4,128]{1,0:T(4,128)(2,1)S(1)}, bf16[4,128]{1,0:T(4,128)(2,1)}, u32[]{:S(2)}) copy-start(bf16[4,128]{1,0:T(4,128)(2,1)} %key_ref.1) | copy-start | bytes 3076
  16.4 13.1 %copy-start.6 = (bf16[4,128]{1,0:T(4,128)(2,1)S(1)}, bf16[4,128]{1,0:T(4,128)(2,1)}, u32[]{:S(2)}) copy-start(bf16[4,128]{1,0:T(4,128)(2,1)} %value_ref.1) | copy-start | bytes 3076
  30.4 4.0 %collective-permute-start = (bf16[4,4,512]{2,1,0:T(4,128)(2,1)S(1)}, bf16[4,4,512]{2,1,0:T(4,128)(2,1)S(1)}, u32[]{:S(2)}, u32[]{:S(2)}) collective-permute-start(bf16[4,4,512]{2,1,0:T(4,128)(2,1)S(1)} %get-tuple-element.11), channel_id=1, source_target_pairs={{0,1},{1,0},{2,3},{3,2},{4,5},{5,4},{6,7},{7,6},{8,9},{9,8},{10,11... | collective-permute-start | bytes 49160 | tf_op jit(solution)/shard_map/swap_cores/ppermute | solution.py:251
  34.4 4.9 %collective-permute-start.1 = (bf16[4,512]{1,0:T(4,128)(2,1)S(1)}, bf16[4,512]{1,0:T(4,128)(2,1)S(1)}, u32[]{:S(2)}, u32[]{:S(2)}) collective-permute-start(bf16[4,512]{1,0:T(4,128)(2,1)S(1)} %get-tuple-element.14), channel_id=1, source_target_pairs={{0,2},{1,3},{2,4},{3,5},{4,6},{5,7},{6,0},{7,1},{8,10},{9,11},{10,... | collective-permute-start | bytes 12296 | tf_op jit(solution)/shard_map/sum_over_chips/ppermute | solution.py:275
  35.6 4.0 %collective-permute-start.2 = (bf16[4,512]{1,0:T(4,128)(2,1)S(1)}, bf16[4,512]{1,0:T(4,128)(2,1)S(1)}, u32[]{:S(2)}, u32[]{:S(2)}) collective-permute-start(bf16[4,512]{1,0:T(4,128)(2,1)S(1)} %get-tuple-element.15), channel_id=1, source_target_pairs={{0,4},{1,5},{2,6},{3,7},{4,0},{5,1},{6,2},{7,3},{8,12},{9,13},{10,... | collective-permute-start | bytes 12296 | tf_op jit(solution)/shard_map/sum_over_chips/ppermute | solution.py:275
  38.1 2.8 %collective-permute-start.3 = (bf16[4,512]{1,0:T(4,128)(2,1)S(1)}, bf16[4,512]{1,0:T(4,128)(2,1)S(1)}, u32[]{:S(2)}, u32[]{:S(2)}) collective-permute-start(bf16[4,512]{1,0:T(4,128)(2,1)S(1)} %get-tuple-element.16), channel_id=1, source_target_pairs={{0,6},{1,7},{2,0},{3,1},{4,2},{5,3},{6,4},{7,5},{8,14},{9,15},{10,... | collective-permute-start | bytes 12296 | tf_op jit(solution)/shard_map/sum_over_chips/ppermute | solution.py:275

commit v6 on v5

--- a/solution.py
+++ b/solution.py
@@ -13,6 +13,7 @@
 LOW = -1e30
 MIB = 1024 * 1024
 STAT_ROWS = 8
+ROUTES = (((1, 3, 0, 2), 0), ((3, 2, 1, 0), 1), ((2, 0, 3, 1), 0))
 
 
 def same_lane(shape):
@@ -21,8 +22,19 @@
     return row, lane
 
 
-def spread_kernel(q_ref, out_ref):
-    out_ref[...] = jnp.broadcast_to(q_ref[...][None], out_ref.shape)
+def by_head(rows, q_ref):
+    mine = q_ref.shape[0]
+    for h in range(HEADS):
+        rows[pl.ds(h, mine, stride=HEADS), :] = q_ref[:, HEAD * h : HEAD * (h + 1)].astype(
+            jnp.float32
+        )
+    return rows[...]
+
+
+def spread_kernel(q_ref, out_ref, rows):
+    out_ref[...] = jnp.broadcast_to(by_head(rows, q_ref)[None], out_ref.shape).astype(
+        out_ref.dtype
+    )
 
 
 def pass_kernel(q_ref, k_hbm, v_hbm, w_hbm, out_ref):
@@ -35,42 +47,40 @@
 
 
 def partials_kernel(
-    req_ref, blk_ref, len_ref, q_ref, k_ref, v_ref, out_ref, rows, sums, stats, req, req_sem
+    req_ref, blk_ref, len_ref, q_ref, k_ref, v_ref, out_ref, sums, stats, req, req_sem
 ):
-    homes, per_home, width = q_ref.shape
+    homes, cells, _ = q_ref.shape
+    per_home = cells // HEADS
     slots, tokens, _ = k_ref.shape
     copy = pltpu.make_async_copy(req_ref, req, req_sem)
     copy.start()
-    row, lane = same_lane((HEADS, slots))
-    request = columns(req_ref, row == lane)
-    block = columns(blk_ref, row == lane)
-    _, lane = same_lane((HEADS, homes * per_home))
-    chosen = lane.astype(jnp.float32) == request
-    filled = jnp.clip(columns(len_ref, chosen) - tokens * block, 0, tokens).astype(jnp.int32)
-    for i in range(homes):
-        rows[per_home * i : per_home * (i + 1), :] = q_ref[i].astype(jnp.float32)
+    row, lane = same_lane((HEADS * slots, slots))
+    mine = row // HEADS == lane
+    request = columns(req_ref, mine)
+    block = columns(blk_ref, mine)
+    row, lane = same_lane((HEADS * slots, homes * per_home))
+    owned = columns(len_ref, lane.astype(jnp.float32) == request)
+    filled = jnp.clip(owned - tokens * block, 0, tokens).astype(jnp.int32)
+    row, lane = same_lane((HEADS * slots, homes * cells))
+    chosen = lane.astype(jnp.float32) == request * HEADS + (row % HEADS).astype(jnp.float32)
+    gathered = jnp.dot(
+        chosen.astype(jnp.bfloat16), q_ref[...].reshape(homes * cells, HEAD),
+        preferred_element_type=jnp.float32,
+    ).astype(jnp.bfloat16)
     sums[...] = jnp.zeros_like(sums)
     stats[...] = jnp.full_like(stats, LOW)
     token = lax.broadcasted_iota(jnp.int32, (HEADS, tokens), 1)
     rate = 1.0 / math.sqrt(HEAD)
-    gathered = jnp.dot(
-        chosen.astype(jnp.bfloat16), rows[...].astype(jnp.bfloat16),
-        preferred_element_type=jnp.float32,
-    )
-    scores = []
-    for s in range(slots):
-        q = jnp.concatenate(
-            [gathered[s : s + 1, HEAD * h : HEAD * (h + 1)] for h in range(HEADS)], axis=0
+    scores = [
+        lax.dot_general(
+            gathered[HEADS * s : HEADS * (s + 1), :], k_ref[s], (((1,), (1,)), ((), ())),
+            preferred_element_type=jnp.float32,
         )
-        scores.append(
-            lax.dot_general(
-                q.astype(jnp.bfloat16), k_ref[s], (((1,), (1,)), ((), ())),
-                preferred_element_type=jnp.float32,
-            )
-        )
+        for s in range(slots)
+    ]
     peaks, totals, probs = [], [], []
     for s in range(slots):
-        score = jnp.where(token < filled[s : s + 1, :], scores[s], LOW)
+        score = jnp.where(token < filled[HEADS * s : HEADS * (s + 1), :], scores[s], LOW)
         peak = jnp.max(score, axis=1, keepdims=True)
         prob = jnp.exp((score - peak) * rate)
         total = jnp.sum(prob, axis=1, keepdims=True)
@@ -80,7 +90,7 @@
     accs = [
         jnp.dot(probs[s], v_ref[s], preferred_element_type=jnp.float32) for s in range(slots)
     ]
-    names = [jnp.broadcast_to(request[s : s + 1, :], (HEADS, HEAD)) for s in range(slots)]
+    names = [jnp.broadcast_to(request[HEADS * s : HEADS * (s + 1), :], (HEADS, HEAD)) for s in range(slots)]
     tops = []
     for s in range(slots):
         top = peaks[s]
@@ -101,7 +111,6 @@
                 acc = acc + jnp.where(same, accs[o], 0.0)
         sums[req[0, s]] = acc / total
         stats[req[0, s]] = tops[s] + jnp.log(total)
-    cells = per_home * HEADS
     out_ref[:, :cells, :] = sums[...].reshape(homes, cells, HEAD).astype(jnp.bfloat16)
     row, lane = same_lane((homes, cells, HEAD))
     picked = jnp.sum(
@@ -131,15 +140,12 @@
         jnp.ones((HEAD, HEAD), jnp.bfloat16),
         preferred_element_type=jnp.float32,
     ).reshape(homes, cells, HEAD)
-    for h in range(HEADS):
-        rows[pl.ds(h, mine, stride=HEADS), :] = q_ref[:, HEAD * h : HEAD * (h + 1)].astype(
-            jnp.float32
-        )
+    heads = by_head(rows, q_ref)
     keys = key_ref[...].astype(jnp.float32)
     keys = jnp.broadcast_to(keys[:, None, :], (mine, HEADS, HEAD)).reshape(cells, HEAD)
     values = value_ref[...].astype(jnp.float32)
     values = jnp.broadcast_to(values[:, None, :], (mine, HEADS, HEAD)).reshape(cells, HEAD)
-    fresh = jnp.sum(rows[...] * keys, axis=1, keepdims=True) * (1.0 / math.sqrt(HEAD))
+    fresh = jnp.sum(heads * keys, axis=1, keepdims=True) * (1.0 / math.sqrt(HEAD))
     fresh = jnp.broadcast_to(fresh, (cells, HEAD))
     top = jnp.maximum(jnp.max(lse, axis=0), fresh)
     weight = jnp.exp(lse - top[None])
@@ -153,12 +159,22 @@
         [rows[pl.ds(h, mine, stride=HEADS), :] for h in range(HEADS)], axis=1
     ).astype(jnp.bfloat16)
     att_ref[...] = attention
-    project(attention, w_ref, out_ref, 1 - lax.axis_index("tp") % 2)
-
-
-def project(attention, w_ref, out_ref, core):
+    project(attention, w_ref, out_ref, False)
+
+
+def there(order, chip):
+    return sum(jnp.where(chip == i, target, 0) for i, target in enumerate(order))
+
+
+def project(attention, w_ref, out_ref, kept):
     chips, _, width = out_ref.shape
+    me = lax.axis_index("tp")
     for chip in range(chips):
+        crossed = sum(
+            ((there(order, me // 2) == chip).astype(jnp.int32) for order, cross in ROUTES if cross),
+            0,
+        )
+        core = lax.rem(me + crossed + (0 if kept else 1), 2)
         first = pl.multiple_of((2 * chip + core) * width, width)
         out_ref[chip] = jnp.dot(
             attention, w_ref[:, pl.ds(first, width)], preferred_element_type=jnp.float32
@@ -166,15 +182,15 @@
 
 
 def own_kernel(att_ref, w_ref, out_ref):
-    project(att_ref[...], w_ref, out_ref, lax.axis_index("tp") % 2)
+    project(att_ref[...], w_ref, out_ref, True)
 
 
 def add_kernel(got_ref, mine_ref, own_ref, *sent_refs):
     chips = got_ref.shape[0]
     me = lax.axis_index("tp") // 2
     own_ref[...] = mine_ref[me] + got_ref[me].astype(jnp.float32)
-    for k, ref in enumerate(sent_refs):
-        chip = lax.rem(me + k + 1, chips)
+    for (order, _), ref in zip(ROUTES, sent_refs):
+        chip = there(order, me)
         ref[...] = (mine_ref[chip] + got_ref[chip].astype(jnp.float32)).astype(ref.dtype)
 
 
@@ -194,20 +210,21 @@
     homes, parts, queries, incoming_keys, incoming_values, cache_keys, pooled_values,
     lengths, slot_request, slot_block, out_weight,
 ):
-    mine, width = queries.shape
+    mine = queries.shape[0]
     cells = mine * HEADS
     slots = cache_keys.shape[0]
     with jax.named_scope("queries_to_owners"):
         copies = pl.pallas_call(
             spread_kernel,
-            out_shape=jax.ShapeDtypeStruct((homes, mine, width), queries.dtype),
+            out_shape=jax.ShapeDtypeStruct((homes, cells, HEAD), queries.dtype),
             in_specs=[whole()],
             out_specs=whole(),
+            scratch_shapes=[pltpu.VMEM((cells, HEAD), jnp.float32)],
             compiler_params=pltpu.CompilerParams(vmem_limit_bytes=4 * MIB),
         )(queries)
         copies = pl.pallas_call(
             pass_kernel,
-            out_shape=jax.ShapeDtypeStruct((homes, mine, width), queries.dtype),
+            out_shape=jax.ShapeDtypeStruct((homes, cells, HEAD), queries.dtype),
             in_specs=[whole()] + [hbm()] * 3,
             out_specs=whole(),
             compiler_params=pltpu.CompilerParams(vmem_limit_bytes=4 * MIB),
@@ -220,7 +237,6 @@
             in_specs=[whole()] * 6,
             out_specs=whole(),
             scratch_shapes=[
-                pltpu.VMEM((homes * mine, width), jnp.float32),
                 pltpu.VMEM((homes * mine, HEADS, HEAD), jnp.float32),
                 pltpu.VMEM((homes * mine, HEADS, HEAD), jnp.float32),
                 pltpu.SMEM((1, slots), jnp.int32),
@@ -270,8 +286,8 @@
             compiler_params=pltpu.CompilerParams(vmem_limit_bytes=4 * MIB),
         )(swapped, own)
     with jax.named_scope("sum_over_chips"):
-        for k, array in enumerate(sent):
-            moves = [(i, (i + 2 * (k + 1)) % parts) for i in range(parts)]
+        for (order, cross), array in zip(ROUTES, sent):
+            moves = [(i, 2 * order[i // 2] + (i + cross) % 2) for i in range(parts)]
             total = total + lax.ppermute(array, "tp", moves).astype(jnp.float32)
         return total.astype(jnp.bfloat16)
 

time: 42 us -> 41.3 us (0.983)
  waiting for transfers between devices: 1.78 us -> 0.94 us
  starting transfers between devices: 8.03 us -> 8.57 us
    ppermute x3, waiting for transfers between devices: 1.6 us -> 0.75 us  [per_device(): total = total + lax.ppermute(array, 'tp', moves).astype(jnp.float32)]
    ppermute x3, starting transfers between devices: 4.89 us -> 5.42 us  [per_device(): total = total + lax.ppermute(array, 'tp', moves).astype(jnp.float32)]
where the time goes in v6:
time: 41.3 us; the launch traced here: 41.1 us
  blocking collectives  25.7 us (62%)
  starting transfers between devices  8.57 us (21%)
  Pallas kernels  4.46 us (11%)
  waiting for transfers between devices  0.94 us (2%)
  local copies, waits for them, and re-layouts  0.75 us (2%)
  other arithmetic  0.6 us (1%)
    all_to_all x1, blocking collectives, per_device(): query_all = lax.all_to_all(copies, 'group', 0, 0, tiled=True)  15.5 us
    all_to_all x1, blocking collectives, per_device(): got = lax.all_to_all(sent, 'group', 0, 0, tiled=True)  10.1 us
    ppermute x3, starting transfers between devices, per_device(): total = total + lax.ppermute(array, 'tp', moves).astype(jnp.float32)  5.42 us
    ppermute x1, starting transfers between devices, per_device(): swapped = lax.ppermute(other, 'tp', [(i, i ^ 1) for i in range(parts)])  3.14 us
    pallas_call x1, Pallas kernels, per_device(): pl.pallas_call(partials_kernel, out_shape=jax.ShapeDtypeStruct((homes, ce...  2.86 us
    pallas_call x1, Pallas kernels, per_device(): pl.pallas_call(combine_kernel, out_shape=[jax.ShapeDtypeStruct((chips, *p...  0.89 us
  transfers between devices with their start and end apart: 4, of which 3 were waited for; matrix products, arithmetic and copies ran while one was open for 0% of the time, Pallas kernels for 2%

profile of v6, /device:TPU:1, one launch (start us, length us, event | category | flops | bytes accessed | tf_op | source)
XLA Modules:
  0.0 41.1 jit_solution(6080408792192060648)
XLA Ops:
  0.0 0.7 %copy-done.3 = bf16[4,1024]{1,0:T(4,128)(2,1)S(1)} copy-done((bf16[4,1024]{1,0:T(4,128)(2,1)S(1)}, bf16[4,1024]{1,0:T(4,128)(2,1)}, u32[]{:S(2)}) %copy-start.3) | copy-done | bytes 8216
  0.7 0.0 copy-start.1
  0.7 0.0 copy-start.2
  0.7 0.0 copy-start.7
  0.8 0.0 copy-start.8
  0.8 0.0 copy-start.9
  0.8 15.5 %all_to_all.10.q_ref = bf16[16,32,128]{2,1,0:T(8,128)(2,1)S(1)} all-to-all(bf16[16,32,128]{2,1,0:T(8,128)(2,1)S(1)} %queries_to_owners.3), channel_id=1, replica_groups=mesh['group'=16,'tp'=8] {'group'}, dimensions={0} | all-to-all | bytes 262144 | tf_op jit(solution)/shard_map/queries_to_owners/all_to_all | solution.py:232
  16.4 0.0 copy-start
  16.4 0.0 copy-start.4
  16.4 0.0 copy-start.5
  16.4 0.0 copy-start.6
  16.4 2.9 %slot_partials.1 = bf16[16,40,128]{2,1,0:T(8,128)(2,1)S(1)} custom-call(s32[1,6]{1,0:T(1,128)S(1)} %bitcast.3, s32[1,6]{1,0:T(1,128)S(1)} %bitcast.4, s32[1,64]{1,0:T(1,128)S(1)} %bitcast.5, bf16[16,32,128]{2,1,0:T(8,128)(2,1)S(1)} %all_to_all.10.q_ref, bf16[6,4096,128]{2,1,0:T(8,128)(2,1)S(1)} %copy-done.1, bf16[6,4096,128]{2,1,0:T(8,128)(2,1)S(1)} %copy-done.2), custom_call_target="tpu_custom_call" | custom-call | tf_op jit(solution)/shard_map/slot_partials/pallas_call | solution.py:234
  19.3 10.1 %all_to_all.11.got_ref = bf16[16,40,128]{2,1,0:T(8,128)(2,1)S(1)} all-to-all(bf16[16,40,128]{2,1,0:T(8,128)(2,1)S(1)} %slot_partials.1), channel_id=1, replica_groups=mesh['group'=16,'tp'=8] {'group'}, dimensions={0} | all-to-all | bytes 327680 | tf_op jit(solution)/shard_map/partials_to_homes/all_to_all | solution.py:251
  29.4 0.9 %combine_and_project.1 = (bf16[4,4,512]{2,1,0:T(4,128)(2,1)S(1)}, bf16[4,1024]{1,0:T(4,128)(2,1)S(1)}) custom-call(bf16[16,40,128]{2,1,0:T(8,128)(2,1)S(1)} %all_to_all.11.got_ref, bf16[4,1024]{1,0:T(4,128)(2,1)S(1)} %copy-done.4, bf16[4,128]{1,0:T(4,128)(2,1)S(1)} %copy-done.5, bf16[4,128]{1,0:T(4,128)(2,1)S(1)} %copy-done.6, bf16[1024,4096]{1,0:T(8,128)(2,1)S(1)} %copy-done), custom_call_target="tpu_custom_call" | custom-call | tf_op jit(solution)/shard_map/combine_and_project/pallas_call | solution.py:255
  30.3 3.1 %collective-permute-start = (bf16[4,4,512]{2,1,0:T(4,128)(2,1)S(1)}, bf16[4,4,512]{2,1,0:T(4,128)(2,1)S(1)}, u32[]{:S(2)}, u32[]{:S(2)}) collective-permute-start(bf16[4,4,512]{2,1,0:T(4,128)(2,1)S(1)} %get-tuple-element.11), channel_id=1, source_target_pairs={{0,1},{1,0},{2,3},{3,2},{4,5},{5,4},{6,7},{7,6},{8,9},{9,8},{10,11... | collective-permute-start | bytes 49160 | tf_op jit(solution)/shard_map/swap_cores/ppermute | solution.py:267
  33.5 0.7 %project_own.1.mine_ref = f32[4,4,512]{2,1,0:T(4,128)S(1)} custom-call(bf16[4,1024]{1,0:T(4,128)(2,1)S(1)} %get-tuple-element.12.att_ref, bf16[1024,4096]{1,0:T(8,128)(2,1)S(1)} %copy-done), custom_call_target="tpu_custom_call" | custom-call | bytes 4194304 | tf_op jit(solution)/shard_map/project_own/pallas_call | solution.py:269
  34.1 0.2 collective-permute-done.got_ref
  34.3 1.3 %collective-permute-start.1 = (bf16[4,512]{1,0:T(4,128)(2,1)S(1)}, bf16[4,512]{1,0:T(4,128)(2,1)S(1)}, u32[]{:S(2)}, u32[]{:S(2)}) collective-permute-start(bf16[4,512]{1,0:T(4,128)(2,1)S(1)} %get-tuple-element.14), channel_id=1, source_target_pairs={{0,2},{1,3},{2,6},{3,7},{4,0},{5,1},{6,4},{7,5},{8,10},{9,11},{10,... | collective-permute-start | bytes 12296 | tf_op jit(solution)/shard_map/sum_over_chips/ppermute | solution.py:291
  35.6 2.3 %collective-permute-start.2 = (bf16[4,512]{1,0:T(4,128)(2,1)S(1)}, bf16[4,512]{1,0:T(4,128)(2,1)S(1)}, u32[]{:S(2)}, u32[]{:S(2)}) collective-permute-start(bf16[4,512]{1,0:T(4,128)(2,1)S(1)} %get-tuple-element.15), channel_id=1, source_target_pairs={{0,7},{1,6},{2,5},{3,4},{4,3},{5,2},{6,1},{7,0},{8,15},{9,14},{10,... | collective-permute-start | bytes 12296 | tf_op jit(solution)/shard_map/sum_over_chips/ppermute | solution.py:291
  37.9 1.8 %collective-permute-start.3 = (bf16[4,512]{1,0:T(4,128)(2,1)S(1)}, bf16[4,512]{1,0:T(4,128)(2,1)S(1)}, u32[]{:S(2)}, u32[]{:S(2)}) collective-permute-start(bf16[4,512]{1,0:T(4,128)(2,1)S(1)} %get-tuple-element.16), channel_id=1, source_target_pairs={{0,4},{1,5},{2,0},{3,1},{4,6},{5,7},{6,2},{7,3},{8,12},{9,13},{10,... | collective-permute-start | bytes 12296 | tf_op jit(solution)/shard_map/sum_over_chips/ppermute | solution.py:291
  39.8 0.0 collective-permute-done.1
  39.8 0.3 collective-permute-done.2
  40.1 0.4 %collective-permute-done.3 = bf16[4,512]{1,0:T(4,128)(2,1)S(1)} collective-permute-done((bf16[4,512]{1,0:T(4,128)(2,1)S(1)}, bf16[4,512]{1,0:T(4,128)(2,1)S(1)}, u32[]{:S(2)}, u32[]{:S(2)}) %collective-permute-start.3) | collective-permute-done | bytes 4128 | tf_op jit(solution)/shard_map/sum_over_chips/ppermute | solution.py:291
  40.5 0.6 %add_convert_fusion = bf16[4,512]{1,0:T(4,128)(2,1)} fusion(bf16[4,512]{1,0:T(4,128)(2,1)S(1)} %collective-permute-done.3, bf16[4,512]{1,0:T(4,128)(2,1)S(1)} %collective-permute-done.2, f32[4,512]{1,0:T(4,128)S(1)} %get-tuple-element.13, bf16[4,512]{1,0:T(4,128)(2,1)S(1)} %collective-permute-done.1), kind=kLoop, calls=%fused_computation | loop fusion | flops 14336 | bytes 24576 | tf_op jit(solution)/shard_map/sum_over_chips/convert_element_type | solution.py:292
  (13 shorter events, 0.1 us)
Async XLA Ops:
  0.0 0.7 %copy-start.3 = (bf16[4,1024]{1,0:T(4,128)(2,1)S(1)}, bf16[4,1024]{1,0:T(4,128)(2,1)}, u32[]{:S(2)}) copy-start(bf16[4,1024]{1,0:T(4,128)(2,1)} %q_ref.3) | copy-start | bytes 24580
  0.7 15.6 %copy-start.1 = (bf16[6,4096,128]{2,1,0:T(8,128)(2,1)S(1)}, bf16[6,4096,128]{2,1,0:T(8,128)(2,1)}, u32[]{:S(2)}) copy-start(bf16[6,4096,128]{2,1,0:T(8,128)(2,1)} %k_ref.1) | copy-start | bytes 18874372
  0.7 15.6 %copy-start.2 = (bf16[6,4096,128]{2,1,0:T(8,128)(2,1)S(1)}, bf16[6,4096,128]{2,1,0:T(8,128)(2,1)}, u32[]{:S(2)}) copy-start(bf16[6,4096,128]{2,1,0:T(8,128)(2,1)} %v_ref.1) | copy-start | bytes 18874372
  0.7 15.6 %copy-start.7 = (s32[6]{0:T(128)S(1)}, s32[6]{0:T(128)}, u32[]{:S(2)}) copy-start(s32[6]{0:T(128)} %param.15) | copy-start | bytes 76
  0.8 15.6 %copy-start.8 = (s32[6]{0:T(128)S(1)}, s32[6]{0:T(128)}, u32[]{:S(2)}) copy-start(s32[6]{0:T(128)} %param.16) | copy-start | bytes 76
  0.8 15.6 %copy-start.9 = (s32[64]{0:T(128)S(1)}, s32[64]{0:T(128)}, u32[]{:S(2)}) copy-start(s32[64]{0:T(128)} %param.14) | copy-start | bytes 772
  16.4 13.1 %copy-start = (bf16[1024,4096]{1,0:T(8,128)(2,1)S(1)}, bf16[1024,4096]{1,0:T(8,128)(2,1)}, u32[]{:S(2)}) copy-start(bf16[1024,4096]{1,0:T(8,128)(2,1)} %w_ref.3) | copy-start | bytes 25165828
  16.4 13.1 %copy-start.4 = (bf16[4,1024]{1,0:T(4,128)(2,1)S(1)}, bf16[4,1024]{1,0:T(4,128)(2,1)}, u32[]{:S(2)}) copy-start(bf16[4,1024]{1,0:T(4,128)(2,1)} %q_ref.3) | copy-start | bytes 24580
  16.4 13.0 %copy-start.5 = (bf16[4,128]{1,0:T(4,128)(2,1)S(1)}, bf16[4,128]{1,0:T(4,128)(2,1)}, u32[]{:S(2)}) copy-start(bf16[4,128]{1,0:T(4,128)(2,1)} %key_ref.1) | copy-start | bytes 3076
  16.4 13.0 %copy-start.6 = (bf16[4,128]{1,0:T(4,128)(2,1)S(1)}, bf16[4,128]{1,0:T(4,128)(2,1)}, u32[]{:S(2)}) copy-start(bf16[4,128]{1,0:T(4,128)(2,1)} %value_ref.1) | copy-start | bytes 3076
  30.3 4.0 %collective-permute-start = (bf16[4,4,512]{2,1,0:T(4,128)(2,1)S(1)}, bf16[4,4,512]{2,1,0:T(4,128)(2,1)S(1)}, u32[]{:S(2)}, u32[]{:S(2)}) collective-permute-start(bf16[4,4,512]{2,1,0:T(4,128)(2,1)S(1)} %get-tuple-element.11), channel_id=1, source_target_pairs={{0,1},{1,0},{2,3},{3,2},{4,5},{5,4},{6,7},{7,6},{8,9},{9,8},{10,11... | collective-permute-start | bytes 49160 | tf_op jit(solution)/shard_map/swap_cores/ppermute | solution.py:267
  34.3 5.4 %collective-permute-start.1 = (bf16[4,512]{1,0:T(4,128)(2,1)S(1)}, bf16[4,512]{1,0:T(4,128)(2,1)S(1)}, u32[]{:S(2)}, u32[]{:S(2)}) collective-permute-start(bf16[4,512]{1,0:T(4,128)(2,1)S(1)} %get-tuple-element.14), channel_id=1, source_target_pairs={{0,2},{1,3},{2,6},{3,7},{4,0},{5,1},{6,4},{7,5},{8,10},{9,11},{10,... | collective-permute-start | bytes 12296 | tf_op jit(solution)/shard_map/sum_over_chips/ppermute | solution.py:291
  35.6 4.5 %collective-permute-start.2 = (bf16[4,512]{1,0:T(4,128)(2,1)S(1)}, bf16[4,512]{1,0:T(4,128)(2,1)S(1)}, u32[]{:S(2)}, u32[]{:S(2)}) collective-permute-start(bf16[4,512]{1,0:T(4,128)(2,1)S(1)} %get-tuple-element.15), channel_id=1, source_target_pairs={{0,7},{1,6},{2,5},{3,4},{4,3},{5,2},{6,1},{7,0},{8,15},{9,14},{10,... | collective-permute-start | bytes 12296 | tf_op jit(solution)/shard_map/sum_over_chips/ppermute | solution.py:291
  37.9 2.6 %collective-permute-start.3 = (bf16[4,512]{1,0:T(4,128)(2,1)S(1)}, bf16[4,512]{1,0:T(4,128)(2,1)S(1)}, u32[]{:S(2)}, u32[]{:S(2)}) collective-permute-start(bf16[4,512]{1,0:T(4,128)(2,1)S(1)} %get-tuple-element.16), channel_id=1, source_target_pairs={{0,4},{1,5},{2,0},{3,1},{4,6},{5,7},{6,2},{7,3},{8,12},{9,13},{10,... | collective-permute-start | bytes 12296 | tf_op jit(solution)/shard_map/sum_over_chips/ppermute | solution.py:291

commit v7 on v6

--- a/solution.py
+++ b/solution.py
@@ -66,14 +66,15 @@
     gathered = jnp.dot(
         chosen.astype(jnp.bfloat16), q_ref[...].reshape(homes * cells, HEAD),
         preferred_element_type=jnp.float32,
-    ).astype(jnp.bfloat16)
+    )
     sums[...] = jnp.zeros_like(sums)
     stats[...] = jnp.full_like(stats, LOW)
     token = lax.broadcasted_iota(jnp.int32, (HEADS, tokens), 1)
     rate = 1.0 / math.sqrt(HEAD)
     scores = [
         lax.dot_general(
-            gathered[HEADS * s : HEADS * (s + 1), :], k_ref[s], (((1,), (1,)), ((), ())),
+            gathered[HEADS * s : HEADS * (s + 1), :].astype(jnp.bfloat16), k_ref[s],
+            (((1,), (1,)), ((), ())),
             preferred_element_type=jnp.float32,
         )
         for s in range(slots)
@@ -82,11 +83,11 @@
     for s in range(slots):
         score = jnp.where(token < filled[HEADS * s : HEADS * (s + 1), :], scores[s], LOW)
         peak = jnp.max(score, axis=1, keepdims=True)
-        prob = jnp.exp((score - peak) * rate)
-        total = jnp.sum(prob, axis=1, keepdims=True)
+        prob = jnp.exp((score - peak) * rate).astype(jnp.bfloat16)
+        total = jnp.sum(prob.astype(jnp.float32), axis=1, keepdims=True)
         peaks.append(jnp.broadcast_to(peak * rate, (HEADS, HEAD)))
         totals.append(jnp.broadcast_to(total, (HEADS, HEAD)))
-        probs.append(prob.astype(jnp.bfloat16))
+        probs.append(prob)
     accs = [
         jnp.dot(probs[s], v_ref[s], preferred_element_type=jnp.float32) for s in range(slots)
     ]
@@ -192,6 +193,16 @@
     for (order, _), ref in zip(ROUTES, sent_refs):
         chip = there(order, me)
         ref[...] = (mine_ref[chip] + got_ref[chip].astype(jnp.float32)).astype(ref.dtype)
+
+
+def total_kernel(own_ref, a_ref, b_ref, c_ref, out_hbm, held, sem):
+    total = own_ref[...]
+    for ref in (a_ref, b_ref, c_ref):
+        total = total + ref[...].astype(jnp.float32)
+    held[...] = total.astype(held.dtype)
+    copy = pltpu.make_async_copy(held, out_hbm, sem)
+    copy.start()
+    copy.wait()
 
 
 def whole():
@@ -286,10 +297,18 @@
             compiler_params=pltpu.CompilerParams(vmem_limit_bytes=4 * MIB),
         )(swapped, own)
     with jax.named_scope("sum_over_chips"):
+        arrived = []
         for (order, cross), array in zip(ROUTES, sent):
             moves = [(i, 2 * order[i // 2] + (i + cross) % 2) for i in range(parts)]
-            total = total + lax.ppermute(array, "tp", moves).astype(jnp.float32)
-        return total.astype(jnp.bfloat16)
+            arrived.append(lax.ppermute(array, "tp", moves))
+        return pl.pallas_call(
+            total_kernel,
+            out_shape=jax.ShapeDtypeStruct(piece, jnp.bfloat16),
+            in_specs=[whole()] * 4,
+            out_specs=hbm(),
+            scratch_shapes=[pltpu.VMEM(piece, jnp.bfloat16), pltpu.SemaphoreType.DMA],
+            compiler_params=pltpu.CompilerParams(vmem_limit_bytes=4 * MIB),
+        )(total, *arrived)
 
 
 def solution(mesh):

time: 41.3 us -> 41.3 us (level)
  Pallas kernels: 4.46 us -> 5.07 us
  other arithmetic: 0.6 us -> 0 us
    pallas_call x0 -> x1, Pallas kernels: none -> 0.61 us  [per_device(): pl.pallas_call(total_kernel, out_shape=jax.ShapeDtypeStruct(piece, jnp.bf...]
    convert_element_type x1 -> x0, other arithmetic: 0.6 us -> none  [per_device(): return total.astype(jnp.bfloat16)]
where the time goes in v7:
time: 41.3 us; the launch traced here: 41.1 us
  blocking collectives  25.7 us (62%)
  starting transfers between devices  8.57 us (21%)
  Pallas kernels  5.07 us (12%)
  waiting for transfers between devices  0.94 us (2%)
  local copies, waits for them, and re-layouts  0.75 us (2%)
    all_to_all x1, blocking collectives, per_device(): query_all = lax.all_to_all(copies, 'group', 0, 0, tiled=True)  15.5 us
    all_to_all x1, blocking collectives, per_device(): got = lax.all_to_all(sent, 'group', 0, 0, tiled=True)  10.1 us
    ppermute x3, starting transfers between devices, per_device(): arrived.append(lax.ppermute(array, 'tp', moves))  5.42 us
    ppermute x1, starting transfers between devices, per_device(): swapped = lax.ppermute(other, 'tp', [(i, i ^ 1) for i in range(parts)])  3.14 us
    pallas_call x1, Pallas kernels, per_device(): pl.pallas_call(partials_kernel, out_shape=jax.ShapeDtypeStruct((homes, ce...  2.86 us
    pallas_call x1, Pallas kernels, per_device(): pl.pallas_call(combine_kernel, out_shape=[jax.ShapeDtypeStruct((chips, *p...  0.89 us
  transfers between devices with their start and end apart: 4, of which 3 were waited for; matrix products, arithmetic and copies ran while one was open for 0% of the time, Pallas kernels for 2%

profile of v7, /device:TPU:1, one launch (start us, length us, event | category | flops | bytes accessed | tf_op | source)
XLA Modules:
  0.0 41.1 jit_solution(11159971491204046855)
XLA Ops:
  0.0 0.7 %copy-done.3 = bf16[4,1024]{1,0:T(4,128)(2,1)S(1)} copy-done((bf16[4,1024]{1,0:T(4,128)(2,1)S(1)}, bf16[4,1024]{1,0:T(4,128)(2,1)}, u32[]{:S(2)}) %copy-start.3) | copy-done | bytes 8216
  0.7 0.0 copy-start.1
  0.7 0.0 copy-start.2
  0.7 0.0 copy-start.7
  0.8 0.0 copy-start.8
  0.8 0.0 copy-start.9
  0.8 15.5 %all_to_all.10.q_ref = bf16[16,32,128]{2,1,0:T(8,128)(2,1)S(1)} all-to-all(bf16[16,32,128]{2,1,0:T(8,128)(2,1)S(1)} %queries_to_owners.3), channel_id=1, replica_groups=mesh['group'=16,'tp'=8] {'group'}, dimensions={0} | all-to-all | bytes 262144 | tf_op jit(solution)/shard_map/queries_to_owners/all_to_all | solution.py:243
  16.4 0.0 copy-start
  16.4 0.0 copy-start.4
  16.4 0.0 copy-start.5
  16.4 0.0 copy-start.6
  16.4 2.9 %slot_partials.1 = bf16[16,40,128]{2,1,0:T(8,128)(2,1)S(1)} custom-call(s32[1,6]{1,0:T(1,128)S(1)} %bitcast.3, s32[1,6]{1,0:T(1,128)S(1)} %bitcast.4, s32[1,64]{1,0:T(1,128)S(1)} %bitcast.5, bf16[16,32,128]{2,1,0:T(8,128)(2,1)S(1)} %all_to_all.10.q_ref, bf16[6,4096,128]{2,1,0:T(8,128)(2,1)S(1)} %copy-done.1, bf16[6,4096,128]{2,1,0:T(8,128)(2,1)S(1)} %copy-done.2), custom_call_target="tpu_custom_call" | custom-call | tf_op jit(solution)/shard_map/slot_partials/pallas_call | solution.py:245
  19.3 10.1 %all_to_all.11.got_ref = bf16[16,40,128]{2,1,0:T(8,128)(2,1)S(1)} all-to-all(bf16[16,40,128]{2,1,0:T(8,128)(2,1)S(1)} %slot_partials.1), channel_id=1, replica_groups=mesh['group'=16,'tp'=8] {'group'}, dimensions={0} | all-to-all | bytes 327680 | tf_op jit(solution)/shard_map/partials_to_homes/all_to_all | solution.py:262
  29.4 0.9 %combine_and_project.1 = (bf16[4,4,512]{2,1,0:T(4,128)(2,1)S(1)}, bf16[4,1024]{1,0:T(4,128)(2,1)S(1)}) custom-call(bf16[16,40,128]{2,1,0:T(8,128)(2,1)S(1)} %all_to_all.11.got_ref, bf16[4,1024]{1,0:T(4,128)(2,1)S(1)} %copy-done.4, bf16[4,128]{1,0:T(4,128)(2,1)S(1)} %copy-done.5, bf16[4,128]{1,0:T(4,128)(2,1)S(1)} %copy-done.6, bf16[1024,4096]{1,0:T(8,128)(2,1)S(1)} %copy-done), custom_call_target="tpu_custom_call" | custom-call | tf_op jit(solution)/shard_map/combine_and_project/pallas_call | solution.py:266
  30.3 3.1 %collective-permute-start = (bf16[4,4,512]{2,1,0:T(4,128)(2,1)S(1)}, bf16[4,4,512]{2,1,0:T(4,128)(2,1)S(1)}, u32[]{:S(2)}, u32[]{:S(2)}) collective-permute-start(bf16[4,4,512]{2,1,0:T(4,128)(2,1)S(1)} %get-tuple-element.11), channel_id=1, source_target_pairs={{0,1},{1,0},{2,3},{3,2},{4,5},{5,4},{6,7},{7,6},{8,9},{9,8},{10,11... | collective-permute-start | bytes 49160 | tf_op jit(solution)/shard_map/swap_cores/ppermute | solution.py:278
  33.5 0.7 %project_own.1.mine_ref = f32[4,4,512]{2,1,0:T(4,128)S(1)} custom-call(bf16[4,1024]{1,0:T(4,128)(2,1)S(1)} %get-tuple-element.12.att_ref, bf16[1024,4096]{1,0:T(8,128)(2,1)S(1)} %copy-done), custom_call_target="tpu_custom_call" | custom-call | bytes 4194304 | tf_op jit(solution)/shard_map/project_own/pallas_call | solution.py:280
  34.1 0.2 collective-permute-done.got_ref
  34.3 1.3 %collective-permute-start.1 = (bf16[4,512]{1,0:T(4,128)(2,1)S(1)}, bf16[4,512]{1,0:T(4,128)(2,1)S(1)}, u32[]{:S(2)}, u32[]{:S(2)}) collective-permute-start(bf16[4,512]{1,0:T(4,128)(2,1)S(1)} %get-tuple-element.14), channel_id=1, source_target_pairs={{0,2},{1,3},{2,6},{3,7},{4,0},{5,1},{6,4},{7,5},{8,10},{9,11},{10,... | collective-permute-start | bytes 12296 | tf_op jit(solution)/shard_map/sum_over_chips/ppermute | solution.py:303
  35.6 2.3 %collective-permute-start.2 = (bf16[4,512]{1,0:T(4,128)(2,1)S(1)}, bf16[4,512]{1,0:T(4,128)(2,1)S(1)}, u32[]{:S(2)}, u32[]{:S(2)}) collective-permute-start(bf16[4,512]{1,0:T(4,128)(2,1)S(1)} %get-tuple-element.15), channel_id=1, source_target_pairs={{0,7},{1,6},{2,5},{3,4},{4,3},{5,2},{6,1},{7,0},{8,15},{9,14},{10,... | collective-permute-start | bytes 12296 | tf_op jit(solution)/shard_map/sum_over_chips/ppermute | solution.py:303
  37.9 1.8 %collective-permute-start.3 = (bf16[4,512]{1,0:T(4,128)(2,1)S(1)}, bf16[4,512]{1,0:T(4,128)(2,1)S(1)}, u32[]{:S(2)}, u32[]{:S(2)}) collective-permute-start(bf16[4,512]{1,0:T(4,128)(2,1)S(1)} %get-tuple-element.16), channel_id=1, source_target_pairs={{0,4},{1,5},{2,0},{3,1},{4,6},{5,7},{6,2},{7,3},{8,12},{9,13},{10,... | collective-permute-start | bytes 12296 | tf_op jit(solution)/shard_map/sum_over_chips/ppermute | solution.py:303
  39.8 0.0 collective-permute-done.1.a_ref
  39.8 0.3 collective-permute-done.2.b_ref
  40.1 0.4 %collective-permute-done.3.c_ref = bf16[4,512]{1,0:T(4,128)(2,1)S(1)} collective-permute-done((bf16[4,512]{1,0:T(4,128)(2,1)S(1)}, bf16[4,512]{1,0:T(4,128)(2,1)S(1)}, u32[]{:S(2)}, u32[]{:S(2)}) %collective-permute-start.3) | collective-permute-done | bytes 4128 | tf_op jit(solution)/shard_map/sum_over_chips/ppermute | solution.py:303
  40.5 0.6 %sum_over_chips.1 = bf16[4,512]{1,0:T(4,128)(2,1)} custom-call(f32[4,512]{1,0:T(4,128)S(1)} %get-tuple-element.13.own_ref, bf16[4,512]{1,0:T(4,128)(2,1)S(1)} %collective-permute-done.1.a_ref, bf16[4,512]{1,0:T(4,128)(2,1)S(1)} %collective-permute-done.2.b_ref, bf16[4,512]{1,0:T(4,128)(2,1)S(1)} %collective-permute-done.3.c_ref), custom_call_target="tpu_custom_call" | custom-call | tf_op jit(solution)/shard_map/sum_over_chips/pallas_call | solution.py:304
  (13 shorter events, 0.1 us)
Async XLA Ops:
  0.0 0.7 %copy-start.3 = (bf16[4,1024]{1,0:T(4,128)(2,1)S(1)}, bf16[4,1024]{1,0:T(4,128)(2,1)}, u32[]{:S(2)}) copy-start(bf16[4,1024]{1,0:T(4,128)(2,1)} %q_ref.3) | copy-start | bytes 24580
  0.7 15.6 %copy-start.1 = (bf16[6,4096,128]{2,1,0:T(8,128)(2,1)S(1)}, bf16[6,4096,128]{2,1,0:T(8,128)(2,1)}, u32[]{:S(2)}) copy-start(bf16[6,4096,128]{2,1,0:T(8,128)(2,1)} %k_ref.1) | copy-start | bytes 18874372
  0.7 15.6 %copy-start.2 = (bf16[6,4096,128]{2,1,0:T(8,128)(2,1)S(1)}, bf16[6,4096,128]{2,1,0:T(8,128)(2,1)}, u32[]{:S(2)}) copy-start(bf16[6,4096,128]{2,1,0:T(8,128)(2,1)} %v_ref.1) | copy-start | bytes 18874372
  0.7 15.6 %copy-start.7 = (s32[6]{0:T(128)S(1)}, s32[6]{0:T(128)}, u32[]{:S(2)}) copy-start(s32[6]{0:T(128)} %param.15) | copy-start | bytes 76
  0.8 15.6 %copy-start.8 = (s32[6]{0:T(128)S(1)}, s32[6]{0:T(128)}, u32[]{:S(2)}) copy-start(s32[6]{0:T(128)} %param.16) | copy-start | bytes 76
  0.8 15.6 %copy-start.9 = (s32[64]{0:T(128)S(1)}, s32[64]{0:T(128)}, u32[]{:S(2)}) copy-start(s32[64]{0:T(128)} %param.14) | copy-start | bytes 772
  16.4 13.1 %copy-start = (bf16[1024,4096]{1,0:T(8,128)(2,1)S(1)}, bf16[1024,4096]{1,0:T(8,128)(2,1)}, u32[]{:S(2)}) copy-start(bf16[1024,4096]{1,0:T(8,128)(2,1)} %w_ref.3) | copy-start | bytes 25165828
  16.4 13.1 %copy-start.4 = (bf16[4,1024]{1,0:T(4,128)(2,1)S(1)}, bf16[4,1024]{1,0:T(4,128)(2,1)}, u32[]{:S(2)}) copy-start(bf16[4,1024]{1,0:T(4,128)(2,1)} %q_ref.3) | copy-start | bytes 24580
  16.4 13.0 %copy-start.5 = (bf16[4,128]{1,0:T(4,128)(2,1)S(1)}, bf16[4,128]{1,0:T(4,128)(2,1)}, u32[]{:S(2)}) copy-start(bf16[4,128]{1,0:T(4,128)(2,1)} %key_ref.1) | copy-start | bytes 3076
  16.4 13.0 %copy-start.6 = (bf16[4,128]{1,0:T(4,128)(2,1)S(1)}, bf16[4,128]{1,0:T(4,128)(2,1)}, u32[]{:S(2)}) copy-start(bf16[4,128]{1,0:T(4,128)(2,1)} %value_ref.1) | copy-start | bytes 3076
  30.3 4.0 %collective-permute-start = (bf16[4,4,512]{2,1,0:T(4,128)(2,1)S(1)}, bf16[4,4,512]{2,1,0:T(4,128)(2,1)S(1)}, u32[]{:S(2)}, u32[]{:S(2)}) collective-permute-start(bf16[4,4,512]{2,1,0:T(4,128)(2,1)S(1)} %get-tuple-element.11), channel_id=1, source_target_pairs={{0,1},{1,0},{2,3},{3,2},{4,5},{5,4},{6,7},{7,6},{8,9},{9,8},{10,11... | collective-permute-start | bytes 49160 | tf_op jit(solution)/shard_map/swap_cores/ppermute | solution.py:278
  34.3 5.4 %collective-permute-start.1 = (bf16[4,512]{1,0:T(4,128)(2,1)S(1)}, bf16[4,512]{1,0:T(4,128)(2,1)S(1)}, u32[]{:S(2)}, u32[]{:S(2)}) collective-permute-start(bf16[4,512]{1,0:T(4,128)(2,1)S(1)} %get-tuple-element.14), channel_id=1, source_target_pairs={{0,2},{1,3},{2,6},{3,7},{4,0},{5,1},{6,4},{7,5},{8,10},{9,11},{10,... | collective-permute-start | bytes 12296 | tf_op jit(solution)/shard_map/sum_over_chips/ppermute | solution.py:303
  35.6 4.5 %collective-permute-start.2 = (bf16[4,512]{1,0:T(4,128)(2,1)S(1)}, bf16[4,512]{1,0:T(4,128)(2,1)S(1)}, u32[]{:S(2)}, u32[]{:S(2)}) collective-permute-start(bf16[4,512]{1,0:T(4,128)(2,1)S(1)} %get-tuple-element.15), channel_id=1, source_target_pairs={{0,7},{1,6},{2,5},{3,4},{4,3},{5,2},{6,1},{7,0},{8,15},{9,14},{10,... | collective-permute-start | bytes 12296 | tf_op jit(solution)/shard_map/sum_over_chips/ppermute | solution.py:303
  37.9 2.6 %collective-permute-start.3 = (bf16[4,512]{1,0:T(4,128)(2,1)S(1)}, bf16[4,512]{1,0:T(4,128)(2,1)S(1)}, u32[]{:S(2)}, u32[]{:S(2)}) collective-permute-start(bf16[4,512]{1,0:T(4,128)(2,1)S(1)} %get-tuple-element.16), channel_id=1, source_target_pairs={{0,4},{1,5},{2,0},{3,1},{4,6},{5,7},{6,2},{7,3},{8,12},{9,13},{10,... | collective-permute-start | bytes 12296 | tf_op jit(solution)/shard_map/sum_over_chips/ppermute | solution.py:303

commit v8 on v7

--- a/solution.py
+++ b/solution.py
@@ -136,11 +136,7 @@
         got_ref[:, cells : cells + 1, :].astype(jnp.float32), (homes, cells, HEAD)
     )
     spread = jnp.where((lane % cells == row) & (lane < 3 * cells), coded, 0.0)
-    lse = jnp.dot(
-        spread.astype(jnp.bfloat16).reshape(homes * cells, HEAD),
-        jnp.ones((HEAD, HEAD), jnp.bfloat16),
-        preferred_element_type=jnp.float32,
-    ).reshape(homes, cells, HEAD)
+    lse = jnp.broadcast_to(jnp.sum(spread, axis=2, keepdims=True), (homes, cells, HEAD))
     heads = by_head(rows, q_ref)
     keys = key_ref[...].astype(jnp.float32)
     keys = jnp.broadcast_to(keys[:, None, :], (mine, HEADS, HEAD)).reshape(cells, HEAD)

time: 41.3 us -> 41.3 us (level)
  no operation moved by 1% of the time
where the time goes in v8:
time: 41.3 us; the launch traced here: 41.1 us
  blocking collectives  25.7 us (62%)
  starting transfers between devices  8.57 us (21%)
  Pallas kernels  5.04 us (12%)
  waiting for transfers between devices  0.94 us (2%)
  local copies, waits for them, and re-layouts  0.75 us (2%)
    all_to_all x1, blocking collectives, per_device(): query_all = lax.all_to_all(copies, 'group', 0, 0, tiled=True)  15.5 us
    all_to_all x1, blocking collectives, per_device(): got = lax.all_to_all(sent, 'group', 0, 0, tiled=True)  10.1 us
    ppermute x3, starting transfers between devices, per_device(): arrived.append(lax.ppermute(array, 'tp', moves))  5.42 us
    ppermute x1, starting transfers between devices, per_device(): swapped = lax.ppermute(other, 'tp', [(i, i ^ 1) for i in range(parts)])  3.14 us
    pallas_call x1, Pallas kernels, per_device(): pl.pallas_call(partials_kernel, out_shape=jax.ShapeDtypeStruct((homes, ce...  2.86 us
    pallas_call x1, Pallas kernels, per_device(): pl.pallas_call(combine_kernel, out_shape=[jax.ShapeDtypeStruct((chips, *p...  0.86 us
  transfers between devices with their start and end apart: 4, of which 3 were waited for; matrix products, arithmetic and copies ran while one was open for 0% of the time, Pallas kernels for 2%

profile of v8, /device:TPU:1, one launch (start us, length us, event | category | flops | bytes accessed | tf_op | source)
XLA Modules:
  0.0 41.1 jit_solution(13902429557719203152)
XLA Ops:
  0.0 0.7 %copy-done.3 = bf16[4,1024]{1,0:T(4,128)(2,1)S(1)} copy-done((bf16[4,1024]{1,0:T(4,128)(2,1)S(1)}, bf16[4,1024]{1,0:T(4,128)(2,1)}, u32[]{:S(2)}) %copy-start.3) | copy-done | bytes 8216
  0.7 0.0 copy-start.1
  0.7 0.0 copy-start.2
  0.7 0.0 copy-start.7
  0.8 0.0 copy-start.8
  0.8 0.0 copy-start.9
  0.8 15.5 %all_to_all.10.q_ref = bf16[16,32,128]{2,1,0:T(8,128)(2,1)S(1)} all-to-all(bf16[16,32,128]{2,1,0:T(8,128)(2,1)S(1)} %queries_to_owners.3), channel_id=1, replica_groups=mesh['group'=16,'tp'=8] {'group'}, dimensions={0} | all-to-all | bytes 262144 | tf_op jit(solution)/shard_map/queries_to_owners/all_to_all | solution.py:239
  16.4 0.0 copy-start
  16.4 0.0 copy-start.4
  16.4 0.0 copy-start.5
  16.4 0.0 copy-start.6
  16.4 2.9 %slot_partials.1 = bf16[16,40,128]{2,1,0:T(8,128)(2,1)S(1)} custom-call(s32[1,6]{1,0:T(1,128)S(1)} %bitcast.3, s32[1,6]{1,0:T(1,128)S(1)} %bitcast.4, s32[1,64]{1,0:T(1,128)S(1)} %bitcast.5, bf16[16,32,128]{2,1,0:T(8,128)(2,1)S(1)} %all_to_all.10.q_ref, bf16[6,4096,128]{2,1,0:T(8,128)(2,1)S(1)} %copy-done.1, bf16[6,4096,128]{2,1,0:T(8,128)(2,1)S(1)} %copy-done.2), custom_call_target="tpu_custom_call" | custom-call | tf_op jit(solution)/shard_map/slot_partials/pallas_call | solution.py:241
  19.3 10.1 %all_to_all.11.got_ref = bf16[16,40,128]{2,1,0:T(8,128)(2,1)S(1)} all-to-all(bf16[16,40,128]{2,1,0:T(8,128)(2,1)S(1)} %slot_partials.1), channel_id=1, replica_groups=mesh['group'=16,'tp'=8] {'group'}, dimensions={0} | all-to-all | bytes 327680 | tf_op jit(solution)/shard_map/partials_to_homes/all_to_all | solution.py:258
  29.4 0.9 %combine_and_project.1 = (bf16[4,4,512]{2,1,0:T(4,128)(2,1)S(1)}, bf16[4,1024]{1,0:T(4,128)(2,1)S(1)}) custom-call(bf16[16,40,128]{2,1,0:T(8,128)(2,1)S(1)} %all_to_all.11.got_ref, bf16[4,1024]{1,0:T(4,128)(2,1)S(1)} %copy-done.4, bf16[4,128]{1,0:T(4,128)(2,1)S(1)} %copy-done.5, bf16[4,128]{1,0:T(4,128)(2,1)S(1)} %copy-done.6, bf16[1024,4096]{1,0:T(8,128)(2,1)S(1)} %copy-done), custom_call_target="tpu_custom_call" | custom-call | tf_op jit(solution)/shard_map/combine_and_project/pallas_call | solution.py:262
  30.3 3.1 %collective-permute-start = (bf16[4,4,512]{2,1,0:T(4,128)(2,1)S(1)}, bf16[4,4,512]{2,1,0:T(4,128)(2,1)S(1)}, u32[]{:S(2)}, u32[]{:S(2)}) collective-permute-start(bf16[4,4,512]{2,1,0:T(4,128)(2,1)S(1)} %get-tuple-element.11), channel_id=1, source_target_pairs={{0,1},{1,0},{2,3},{3,2},{4,5},{5,4},{6,7},{7,6},{8,9},{9,8},{10,11... | collective-permute-start | bytes 49160 | tf_op jit(solution)/shard_map/swap_cores/ppermute | solution.py:274
  33.4 0.7 %project_own.1.mine_ref = f32[4,4,512]{2,1,0:T(4,128)S(1)} custom-call(bf16[4,1024]{1,0:T(4,128)(2,1)S(1)} %get-tuple-element.12.att_ref, bf16[1024,4096]{1,0:T(8,128)(2,1)S(1)} %copy-done), custom_call_target="tpu_custom_call" | custom-call | bytes 4194304 | tf_op jit(solution)/shard_map/project_own/pallas_call | solution.py:276
  34.1 0.2 collective-permute-done.got_ref
  34.3 1.3 %collective-permute-start.1 = (bf16[4,512]{1,0:T(4,128)(2,1)S(1)}, bf16[4,512]{1,0:T(4,128)(2,1)S(1)}, u32[]{:S(2)}, u32[]{:S(2)}) collective-permute-start(bf16[4,512]{1,0:T(4,128)(2,1)S(1)} %get-tuple-element.14), channel_id=1, source_target_pairs={{0,2},{1,3},{2,6},{3,7},{4,0},{5,1},{6,4},{7,5},{8,10},{9,11},{10,... | collective-permute-start | bytes 12296 | tf_op jit(solution)/shard_map/sum_over_chips/ppermute | solution.py:299
  35.6 2.3 %collective-permute-start.2 = (bf16[4,512]{1,0:T(4,128)(2,1)S(1)}, bf16[4,512]{1,0:T(4,128)(2,1)S(1)}, u32[]{:S(2)}, u32[]{:S(2)}) collective-permute-start(bf16[4,512]{1,0:T(4,128)(2,1)S(1)} %get-tuple-element.15), channel_id=1, source_target_pairs={{0,7},{1,6},{2,5},{3,4},{4,3},{5,2},{6,1},{7,0},{8,15},{9,14},{10,... | collective-permute-start | bytes 12296 | tf_op jit(solution)/shard_map/sum_over_chips/ppermute | solution.py:299
  37.9 1.8 %collective-permute-start.3 = (bf16[4,512]{1,0:T(4,128)(2,1)S(1)}, bf16[4,512]{1,0:T(4,128)(2,1)S(1)}, u32[]{:S(2)}, u32[]{:S(2)}) collective-permute-start(bf16[4,512]{1,0:T(4,128)(2,1)S(1)} %get-tuple-element.16), channel_id=1, source_target_pairs={{0,4},{1,5},{2,0},{3,1},{4,6},{5,7},{6,2},{7,3},{8,12},{9,13},{10,... | collective-permute-start | bytes 12296 | tf_op jit(solution)/shard_map/sum_over_chips/ppermute | solution.py:299
  39.7 0.0 collective-permute-done.1.a_ref
  39.7 0.3 collective-permute-done.2.b_ref
  40.1 0.4 %collective-permute-done.3.c_ref = bf16[4,512]{1,0:T(4,128)(2,1)S(1)} collective-permute-done((bf16[4,512]{1,0:T(4,128)(2,1)S(1)}, bf16[4,512]{1,0:T(4,128)(2,1)S(1)}, u32[]{:S(2)}, u32[]{:S(2)}) %collective-permute-start.3) | collective-permute-done | bytes 4128 | tf_op jit(solution)/shard_map/sum_over_chips/ppermute | solution.py:299
  40.5 0.6 %sum_over_chips.1 = bf16[4,512]{1,0:T(4,128)(2,1)} custom-call(f32[4,512]{1,0:T(4,128)S(1)} %get-tuple-element.13.own_ref, bf16[4,512]{1,0:T(4,128)(2,1)S(1)} %collective-permute-done.1.a_ref, bf16[4,512]{1,0:T(4,128)(2,1)S(1)} %collective-permute-done.2.b_ref, bf16[4,512]{1,0:T(4,128)(2,1)S(1)} %collective-permute-done.3.c_ref), custom_call_target="tpu_custom_call" | custom-call | tf_op jit(solution)/shard_map/sum_over_chips/pallas_call | solution.py:300
  (13 shorter events, 0.1 us)
Async XLA Ops:
  0.0 0.7 %copy-start.3 = (bf16[4,1024]{1,0:T(4,128)(2,1)S(1)}, bf16[4,1024]{1,0:T(4,128)(2,1)}, u32[]{:S(2)}) copy-start(bf16[4,1024]{1,0:T(4,128)(2,1)} %q_ref.3) | copy-start | bytes 24580
  0.7 15.6 %copy-start.1 = (bf16[6,4096,128]{2,1,0:T(8,128)(2,1)S(1)}, bf16[6,4096,128]{2,1,0:T(8,128)(2,1)}, u32[]{:S(2)}) copy-start(bf16[6,4096,128]{2,1,0:T(8,128)(2,1)} %k_ref.1) | copy-start | bytes 18874372
  0.7 15.6 %copy-start.2 = (bf16[6,4096,128]{2,1,0:T(8,128)(2,1)S(1)}, bf16[6,4096,128]{2,1,0:T(8,128)(2,1)}, u32[]{:S(2)}) copy-start(bf16[6,4096,128]{2,1,0:T(8,128)(2,1)} %v_ref.1) | copy-start | bytes 18874372
  0.7 15.6 %copy-start.7 = (s32[6]{0:T(128)S(1)}, s32[6]{0:T(128)}, u32[]{:S(2)}) copy-start(s32[6]{0:T(128)} %param.15) | copy-start | bytes 76
  0.8 15.6 %copy-start.8 = (s32[6]{0:T(128)S(1)}, s32[6]{0:T(128)}, u32[]{:S(2)}) copy-start(s32[6]{0:T(128)} %param.16) | copy-start | bytes 76
  0.8 15.6 %copy-start.9 = (s32[64]{0:T(128)S(1)}, s32[64]{0:T(128)}, u32[]{:S(2)}) copy-start(s32[64]{0:T(128)} %param.14) | copy-start | bytes 772
  16.4 13.1 %copy-start = (bf16[1024,4096]{1,0:T(8,128)(2,1)S(1)}, bf16[1024,4096]{1,0:T(8,128)(2,1)}, u32[]{:S(2)}) copy-start(bf16[1024,4096]{1,0:T(8,128)(2,1)} %w_ref.3) | copy-start | bytes 25165828
  16.4 13.1 %copy-start.4 = (bf16[4,1024]{1,0:T(4,128)(2,1)S(1)}, bf16[4,1024]{1,0:T(4,128)(2,1)}, u32[]{:S(2)}) copy-start(bf16[4,1024]{1,0:T(4,128)(2,1)} %q_ref.3) | copy-start | bytes 24580
  16.4 13.0 %copy-start.5 = (bf16[4,128]{1,0:T(4,128)(2,1)S(1)}, bf16[4,128]{1,0:T(4,128)(2,1)}, u32[]{:S(2)}) copy-start(bf16[4,128]{1,0:T(4,128)(2,1)} %key_ref.1) | copy-start | bytes 3076
  16.4 13.0 %copy-start.6 = (bf16[4,128]{1,0:T(4,128)(2,1)S(1)}, bf16[4,128]{1,0:T(4,128)(2,1)}, u32[]{:S(2)}) copy-start(bf16[4,128]{1,0:T(4,128)(2,1)} %value_ref.1) | copy-start | bytes 3076
  30.3 4.0 %collective-permute-start = (bf16[4,4,512]{2,1,0:T(4,128)(2,1)S(1)}, bf16[4,4,512]{2,1,0:T(4,128)(2,1)S(1)}, u32[]{:S(2)}, u32[]{:S(2)}) collective-permute-start(bf16[4,4,512]{2,1,0:T(4,128)(2,1)S(1)} %get-tuple-element.11), channel_id=1, source_target_pairs={{0,1},{1,0},{2,3},{3,2},{4,5},{5,4},{6,7},{7,6},{8,9},{9,8},{10,11... | collective-permute-start | bytes 49160 | tf_op jit(solution)/shard_map/swap_cores/ppermute | solution.py:274
  34.3 5.4 %collective-permute-start.1 = (bf16[4,512]{1,0:T(4,128)(2,1)S(1)}, bf16[4,512]{1,0:T(4,128)(2,1)S(1)}, u32[]{:S(2)}, u32[]{:S(2)}) collective-permute-start(bf16[4,512]{1,0:T(4,128)(2,1)S(1)} %get-tuple-element.14), channel_id=1, source_target_pairs={{0,2},{1,3},{2,6},{3,7},{4,0},{5,1},{6,4},{7,5},{8,10},{9,11},{10,... | collective-permute-start | bytes 12296 | tf_op jit(solution)/shard_map/sum_over_chips/ppermute | solution.py:299
  35.6 4.5 %collective-permute-start.2 = (bf16[4,512]{1,0:T(4,128)(2,1)S(1)}, bf16[4,512]{1,0:T(4,128)(2,1)S(1)}, u32[]{:S(2)}, u32[]{:S(2)}) collective-permute-start(bf16[4,512]{1,0:T(4,128)(2,1)S(1)} %get-tuple-element.15), channel_id=1, source_target_pairs={{0,7},{1,6},{2,5},{3,4},{4,3},{5,2},{6,1},{7,0},{8,15},{9,14},{10,... | collective-permute-start | bytes 12296 | tf_op jit(solution)/shard_map/sum_over_chips/ppermute | solution.py:299
  37.9 2.6 %collective-permute-start.3 = (bf16[4,512]{1,0:T(4,128)(2,1)S(1)}, bf16[4,512]{1,0:T(4,128)(2,1)S(1)}, u32[]{:S(2)}, u32[]{:S(2)}) collective-permute-start(bf16[4,512]{1,0:T(4,128)(2,1)S(1)} %get-tuple-element.16), channel_id=1, source_target_pairs={{0,4},{1,5},{2,0},{3,1},{4,6},{5,7},{6,2},{7,3},{8,12},{9,13},{10,... | collective-permute-start | bytes 12296 | tf_op jit(solution)/shard_map/sum_over_chips/ppermute | solution.py:299

commit v9 on v8

--- a/solution.py
+++ b/solution.py
@@ -32,8 +32,8 @@
 
 
 def spread_kernel(q_ref, out_ref, rows):
-    out_ref[...] = jnp.broadcast_to(by_head(rows, q_ref)[None], out_ref.shape).astype(
-        out_ref.dtype
+    out_ref[...] = jnp.broadcast_to(
+        by_head(rows, q_ref).astype(out_ref.dtype)[None], out_ref.shape
     )
 
 

time: 41.3 us -> 41.3 us (level)
  no operation moved by 1% of the time
where the time goes in v9:
time: 41.3 us; the launch traced here: 41.1 us
  blocking collectives  25.7 us (62%)
  starting transfers between devices  8.57 us (21%)
  Pallas kernels  5.04 us (12%)
  waiting for transfers between devices  0.94 us (2%)
  local copies, waits for them, and re-layouts  0.75 us (2%)
    all_to_all x1, blocking collectives, per_device(): query_all = lax.all_to_all(copies, 'group', 0, 0, tiled=True)  15.5 us
    all_to_all x1, blocking collectives, per_device(): got = lax.all_to_all(sent, 'group', 0, 0, tiled=True)  10.1 us
    ppermute x3, starting transfers between devices, per_device(): arrived.append(lax.ppermute(array, 'tp', moves))  5.42 us
    ppermute x1, starting transfers between devices, per_device(): swapped = lax.ppermute(other, 'tp', [(i, i ^ 1) for i in range(parts)])  3.14 us
    pallas_call x1, Pallas kernels, per_device(): pl.pallas_call(partials_kernel, out_shape=jax.ShapeDtypeStruct((homes, ce...  2.86 us
    pallas_call x1, Pallas kernels, per_device(): pl.pallas_call(combine_kernel, out_shape=[jax.ShapeDtypeStruct((chips, *p...  0.86 us
  transfers between devices with their start and end apart: 4, of which 3 were waited for; matrix products, arithmetic and copies ran while one was open for 0% of the time, Pallas kernels for 2%

profile of v9, /device:TPU:1, one launch (start us, length us, event | category | flops | bytes accessed | tf_op | source)
XLA Modules:
  0.0 41.1 jit_solution(13902429557719203152)
XLA Ops:
  0.0 0.7 %copy-done.3 = bf16[4,1024]{1,0:T(4,128)(2,1)S(1)} copy-done((bf16[4,1024]{1,0:T(4,128)(2,1)S(1)}, bf16[4,1024]{1,0:T(4,128)(2,1)}, u32[]{:S(2)}) %copy-start.3) | copy-done | bytes 8216
  0.7 0.0 copy-start.1
  0.7 0.0 copy-start.2
  0.7 0.0 copy-start.7
  0.8 0.0 copy-start.8
  0.8 0.0 copy-start.9
  0.8 15.5 %all_to_all.10.q_ref = bf16[16,32,128]{2,1,0:T(8,128)(2,1)S(1)} all-to-all(bf16[16,32,128]{2,1,0:T(8,128)(2,1)S(1)} %queries_to_owners.3), channel_id=1, replica_groups=mesh['group'=16,'tp'=8] {'group'}, dimensions={0} | all-to-all | bytes 262144 | tf_op jit(solution)/shard_map/queries_to_owners/all_to_all | solution.py:239
  16.4 0.0 copy-start
  16.4 0.0 copy-start.4
  16.4 0.0 copy-start.5
  16.4 0.0 copy-start.6
  16.4 2.9 %slot_partials.1 = bf16[16,40,128]{2,1,0:T(8,128)(2,1)S(1)} custom-call(s32[1,6]{1,0:T(1,128)S(1)} %bitcast.3, s32[1,6]{1,0:T(1,128)S(1)} %bitcast.4, s32[1,64]{1,0:T(1,128)S(1)} %bitcast.5, bf16[16,32,128]{2,1,0:T(8,128)(2,1)S(1)} %all_to_all.10.q_ref, bf16[6,4096,128]{2,1,0:T(8,128)(2,1)S(1)} %copy-done.1, bf16[6,4096,128]{2,1,0:T(8,128)(2,1)S(1)} %copy-done.2), custom_call_target="tpu_custom_call" | custom-call | tf_op jit(solution)/shard_map/slot_partials/pallas_call | solution.py:241
  19.3 10.1 %all_to_all.11.got_ref = bf16[16,40,128]{2,1,0:T(8,128)(2,1)S(1)} all-to-all(bf16[16,40,128]{2,1,0:T(8,128)(2,1)S(1)} %slot_partials.1), channel_id=1, replica_groups=mesh['group'=16,'tp'=8] {'group'}, dimensions={0} | all-to-all | bytes 327680 | tf_op jit(solution)/shard_map/partials_to_homes/all_to_all | solution.py:258
  29.4 0.9 %combine_and_project.1 = (bf16[4,4,512]{2,1,0:T(4,128)(2,1)S(1)}, bf16[4,1024]{1,0:T(4,128)(2,1)S(1)}) custom-call(bf16[16,40,128]{2,1,0:T(8,128)(2,1)S(1)} %all_to_all.11.got_ref, bf16[4,1024]{1,0:T(4,128)(2,1)S(1)} %copy-done.4, bf16[4,128]{1,0:T(4,128)(2,1)S(1)} %copy-done.5, bf16[4,128]{1,0:T(4,128)(2,1)S(1)} %copy-done.6, bf16[1024,4096]{1,0:T(8,128)(2,1)S(1)} %copy-done), custom_call_target="tpu_custom_call" | custom-call | tf_op jit(solution)/shard_map/combine_and_project/pallas_call | solution.py:262
  30.3 3.1 %collective-permute-start = (bf16[4,4,512]{2,1,0:T(4,128)(2,1)S(1)}, bf16[4,4,512]{2,1,0:T(4,128)(2,1)S(1)}, u32[]{:S(2)}, u32[]{:S(2)}) collective-permute-start(bf16[4,4,512]{2,1,0:T(4,128)(2,1)S(1)} %get-tuple-element.11), channel_id=1, source_target_pairs={{0,1},{1,0},{2,3},{3,2},{4,5},{5,4},{6,7},{7,6},{8,9},{9,8},{10,11... | collective-permute-start | bytes 49160 | tf_op jit(solution)/shard_map/swap_cores/ppermute | solution.py:274
  33.4 0.7 %project_own.1.mine_ref = f32[4,4,512]{2,1,0:T(4,128)S(1)} custom-call(bf16[4,1024]{1,0:T(4,128)(2,1)S(1)} %get-tuple-element.12.att_ref, bf16[1024,4096]{1,0:T(8,128)(2,1)S(1)} %copy-done), custom_call_target="tpu_custom_call" | custom-call | bytes 4194304 | tf_op jit(solution)/shard_map/project_own/pallas_call | solution.py:276
  34.1 0.2 collective-permute-done.got_ref
  34.3 1.3 %collective-permute-start.1 = (bf16[4,512]{1,0:T(4,128)(2,1)S(1)}, bf16[4,512]{1,0:T(4,128)(2,1)S(1)}, u32[]{:S(2)}, u32[]{:S(2)}) collective-permute-start(bf16[4,512]{1,0:T(4,128)(2,1)S(1)} %get-tuple-element.14), channel_id=1, source_target_pairs={{0,2},{1,3},{2,6},{3,7},{4,0},{5,1},{6,4},{7,5},{8,10},{9,11},{10,... | collective-permute-start | bytes 12296 | tf_op jit(solution)/shard_map/sum_over_chips/ppermute | solution.py:299
  35.6 2.3 %collective-permute-start.2 = (bf16[4,512]{1,0:T(4,128)(2,1)S(1)}, bf16[4,512]{1,0:T(4,128)(2,1)S(1)}, u32[]{:S(2)}, u32[]{:S(2)}) collective-permute-start(bf16[4,512]{1,0:T(4,128)(2,1)S(1)} %get-tuple-element.15), channel_id=1, source_target_pairs={{0,7},{1,6},{2,5},{3,4},{4,3},{5,2},{6,1},{7,0},{8,15},{9,14},{10,... | collective-permute-start | bytes 12296 | tf_op jit(solution)/shard_map/sum_over_chips/ppermute | solution.py:299
  37.9 1.8 %collective-permute-start.3 = (bf16[4,512]{1,0:T(4,128)(2,1)S(1)}, bf16[4,512]{1,0:T(4,128)(2,1)S(1)}, u32[]{:S(2)}, u32[]{:S(2)}) collective-permute-start(bf16[4,512]{1,0:T(4,128)(2,1)S(1)} %get-tuple-element.16), channel_id=1, source_target_pairs={{0,4},{1,5},{2,0},{3,1},{4,6},{5,7},{6,2},{7,3},{8,12},{9,13},{10,... | collective-permute-start | bytes 12296 | tf_op jit(solution)/shard_map/sum_over_chips/ppermute | solution.py:299
  39.7 0.0 collective-permute-done.1.a_ref
  39.7 0.3 collective-permute-done.2.b_ref
  40.1 0.4 %collective-permute-done.3.c_ref = bf16[4,512]{1,0:T(4,128)(2,1)S(1)} collective-permute-done((bf16[4,512]{1,0:T(4,128)(2,1)S(1)}, bf16[4,512]{1,0:T(4,128)(2,1)S(1)}, u32[]{:S(2)}, u32[]{:S(2)}) %collective-permute-start.3) | collective-permute-done | bytes 4128 | tf_op jit(solution)/shard_map/sum_over_chips/ppermute | solution.py:299
  40.5 0.6 %sum_over_chips.1 = bf16[4,512]{1,0:T(4,128)(2,1)} custom-call(f32[4,512]{1,0:T(4,128)S(1)} %get-tuple-element.13.own_ref, bf16[4,512]{1,0:T(4,128)(2,1)S(1)} %collective-permute-done.1.a_ref, bf16[4,512]{1,0:T(4,128)(2,1)S(1)} %collective-permute-done.2.b_ref, bf16[4,512]{1,0:T(4,128)(2,1)S(1)} %collective-permute-done.3.c_ref), custom_call_target="tpu_custom_call" | custom-call | tf_op jit(solution)/shard_map/sum_over_chips/pallas_call | solution.py:300
  (13 shorter events, 0.1 us)
Async XLA Ops:
  0.0 0.7 %copy-start.3 = (bf16[4,1024]{1,0:T(4,128)(2,1)S(1)}, bf16[4,1024]{1,0:T(4,128)(2,1)}, u32[]{:S(2)}) copy-start(bf16[4,1024]{1,0:T(4,128)(2,1)} %q_ref.3) | copy-start | bytes 24580
  0.7 15.6 %copy-start.1 = (bf16[6,4096,128]{2,1,0:T(8,128)(2,1)S(1)}, bf16[6,4096,128]{2,1,0:T(8,128)(2,1)}, u32[]{:S(2)}) copy-start(bf16[6,4096,128]{2,1,0:T(8,128)(2,1)} %k_ref.1) | copy-start | bytes 18874372
  0.7 15.6 %copy-start.2 = (bf16[6,4096,128]{2,1,0:T(8,128)(2,1)S(1)}, bf16[6,4096,128]{2,1,0:T(8,128)(2,1)}, u32[]{:S(2)}) copy-start(bf16[6,4096,128]{2,1,0:T(8,128)(2,1)} %v_ref.1) | copy-start | bytes 18874372
  0.7 15.6 %copy-start.7 = (s32[6]{0:T(128)S(1)}, s32[6]{0:T(128)}, u32[]{:S(2)}) copy-start(s32[6]{0:T(128)} %param.15) | copy-start | bytes 76
  0.8 15.6 %copy-start.8 = (s32[6]{0:T(128)S(1)}, s32[6]{0:T(128)}, u32[]{:S(2)}) copy-start(s32[6]{0:T(128)} %param.16) | copy-start | bytes 76
  0.8 15.6 %copy-start.9 = (s32[64]{0:T(128)S(1)}, s32[64]{0:T(128)}, u32[]{:S(2)}) copy-start(s32[64]{0:T(128)} %param.14) | copy-start | bytes 772
  16.4 13.1 %copy-start = (bf16[1024,4096]{1,0:T(8,128)(2,1)S(1)}, bf16[1024,4096]{1,0:T(8,128)(2,1)}, u32[]{:S(2)}) copy-start(bf16[1024,4096]{1,0:T(8,128)(2,1)} %w_ref.3) | copy-start | bytes 25165828
  16.4 13.1 %copy-start.4 = (bf16[4,1024]{1,0:T(4,128)(2,1)S(1)}, bf16[4,1024]{1,0:T(4,128)(2,1)}, u32[]{:S(2)}) copy-start(bf16[4,1024]{1,0:T(4,128)(2,1)} %q_ref.3) | copy-start | bytes 24580
  16.4 13.0 %copy-start.5 = (bf16[4,128]{1,0:T(4,128)(2,1)S(1)}, bf16[4,128]{1,0:T(4,128)(2,1)}, u32[]{:S(2)}) copy-start(bf16[4,128]{1,0:T(4,128)(2,1)} %key_ref.1) | copy-start | bytes 3076
  16.4 13.0 %copy-start.6 = (bf16[4,128]{1,0:T(4,128)(2,1)S(1)}, bf16[4,128]{1,0:T(4,128)(2,1)}, u32[]{:S(2)}) copy-start(bf16[4,128]{1,0:T(4,128)(2,1)} %value_ref.1) | copy-start | bytes 3076
  30.3 4.0 %collective-permute-start = (bf16[4,4,512]{2,1,0:T(4,128)(2,1)S(1)}, bf16[4,4,512]{2,1,0:T(4,128)(2,1)S(1)}, u32[]{:S(2)}, u32[]{:S(2)}) collective-permute-start(bf16[4,4,512]{2,1,0:T(4,128)(2,1)S(1)} %get-tuple-element.11), channel_id=1, source_target_pairs={{0,1},{1,0},{2,3},{3,2},{4,5},{5,4},{6,7},{7,6},{8,9},{9,8},{10,11... | collective-permute-start | bytes 49160 | tf_op jit(solution)/shard_map/swap_cores/ppermute | solution.py:274
  34.3 5.4 %collective-permute-start.1 = (bf16[4,512]{1,0:T(4,128)(2,1)S(1)}, bf16[4,512]{1,0:T(4,128)(2,1)S(1)}, u32[]{:S(2)}, u32[]{:S(2)}) collective-permute-start(bf16[4,512]{1,0:T(4,128)(2,1)S(1)} %get-tuple-element.14), channel_id=1, source_target_pairs={{0,2},{1,3},{2,6},{3,7},{4,0},{5,1},{6,4},{7,5},{8,10},{9,11},{10,... | collective-permute-start | bytes 12296 | tf_op jit(solution)/shard_map/sum_over_chips/ppermute | solution.py:299
  35.6 4.5 %collective-permute-start.2 = (bf16[4,512]{1,0:T(4,128)(2,1)S(1)}, bf16[4,512]{1,0:T(4,128)(2,1)S(1)}, u32[]{:S(2)}, u32[]{:S(2)}) collective-permute-start(bf16[4,512]{1,0:T(4,128)(2,1)S(1)} %get-tuple-element.15), channel_id=1, source_target_pairs={{0,7},{1,6},{2,5},{3,4},{4,3},{5,2},{6,1},{7,0},{8,15},{9,14},{10,... | collective-permute-start | bytes 12296 | tf_op jit(solution)/shard_map/sum_over_chips/ppermute | solution.py:299
  37.9 2.6 %collective-permute-start.3 = (bf16[4,512]{1,0:T(4,128)(2,1)S(1)}, bf16[4,512]{1,0:T(4,128)(2,1)S(1)}, u32[]{:S(2)}, u32[]{:S(2)}) collective-permute-start(bf16[4,512]{1,0:T(4,128)(2,1)S(1)} %get-tuple-element.16), channel_id=1, source_target_pairs={{0,4},{1,5},{2,0},{3,1},{4,6},{5,7},{6,2},{7,3},{8,12},{9,13},{10,... | collective-permute-start | bytes 12296 | tf_op jit(solution)/shard_map/sum_over_chips/ppermute | solution.py:299
